TPU v7x, 32 devices: a whole 2x2x4 slice. The times are simulated.
32 devices in a mesh: ctx: 8 (over z, core), head: 4 (over y, x).
Axes of the slice: x: 2, y: 2, z: 4, core: 2. Of those that a mesh axis runs over, the one named last changes fastest.
Arguments:
- hidden: bfloat16 [4096, 4096], P('ctx'), may hold values from -6 to 6
- base_ids: int32 [4096], P('ctx'), may hold values from 0 to 4
- norm_gain: float32 [4096], replicated, may hold values from 0.1 to 1.9
- w_gate: bfloat16 [4096, 4096], P(None, 'head'), may hold values from -0.09375 to 0.09375
- w_value: bfloat16 [4096, 4096], P(None, 'head'), may hold values from -0.09375 to 0.09375
- w_bc: bfloat16 [4096, 256], replicated, may hold values from -0.09375 to 0.09375
- w_step: bfloat16 [4096, 64], P(None, 'head'), may hold values from -0.09375 to 0.09375
- conv_value: float32 [4, 4096], P(None, 'head'), may hold values from -3 to 3
- conv_bc: float32 [4, 256], replicated, may hold values from -3 to 3
- step_bias: float32 [64], P('head'), may hold values from -5.5 to -3.5
- decay_rate: float32 [64], P('head'), as said below
- skip_gain: float32 [64], P('head'), may hold values from 0.5 to 1.5
- out_gain: float32 [4096], P('head'), may hold values from 0.1 to 1.9
- w_out: bfloat16 [4096, 4096], P('head'), may hold values from -0.09375 to 0.09375
Outputs:
- mixed_out: bfloat16 [4096, 4096], P('ctx', 'head')
Inputs may be any that keep to these rules, and one draw needn't show every extreme that they name: `base_ids`: 4 marks an unknown base N, 0 to 3 are A, C, G, T. `decay_rate`: positive rates.
All inputs are finite; a program needn't handle non-finite values.
Results may differ from a plain program's by a relative error of at most 0.0059.
Values may be sent and summed in bfloat16 or wider, within the bound.
A program may use at most 192 MiB of HBM per device.

v0:
```python
import jax
import jax.numpy as jnp
from jax import lax
from jax.sharding import PartitionSpec as P

CONV_WIDTH = 4
BLOCK = 256


EPSILON = 1e-05
PRECISE = lax.Precision.HIGHEST


def swapped(array, axis, stride):
    return lax.ppermute(array, axis, [(i, i ^ 1 << stride) for i in range(lax.axis_size(axis))])


def padded_2(array, sides, width):
    for axis, dim in sides:
        size, length = (lax.axis_size(axis), array.shape[dim])
        up = [(i, (i + 1) % size) for i in range(size - 1)]
        down = [(j, i) for i, j in up]
        last = lax.slice_in_dim(array, length - width, length, axis=dim)
        initial = lax.slice_in_dim(array, 0, width, axis=dim)
        before = lax.ppermute(last, axis, up)
        after = lax.ppermute(initial, axis, down)
        array = jnp.concatenate([before, array, after], axis=dim)
    return array


def prefix(part, axis, combine, identity, reverse):
    count = lax.axis_size(axis)
    place = lax.axis_index(axis)
    ahead = count - 1 - place if reverse else place
    gathered = jax.tree.map(lambda a: lax.all_gather(a, axis), part)
    state = jax.tree.map(lambda a, e: jnp.zeros_like(a) + jnp.asarray(e, a.dtype), part, identity)

    def one(lap, state):
        source = count - 1 - lap if reverse else lap
        return combine(
            state, jax.tree.map(lambda a: lax.dynamic_index_in_dim(a, source, 0, False), gathered)
        )

    return lax.fori_loop(0, ahead, one, state)


def convolve(padded, kernel, kernel_len):
    length = padded.shape[1] - 2 * (kernel_len - 1)
    reach = 2 * (kernel_len - 1)
    forward_sum = kernel[0] * padded[:, 0:length]
    backward_sum = kernel[0] * padded[:, reach : reach + length]
    for offset in range(1, kernel_len):
        forward_sum = forward_sum + kernel[offset] * padded[:, offset : offset + length]
        backward_sum = (
            backward_sum + kernel[offset] * padded[:, reach - offset : reach - offset + length]
        )
    return (forward_sum, backward_sum)


def lane_flip(source_array):
    return jnp.concatenate([source_array[:2], source_array[2:, ::-1]], axis=0)


def local_scan(values, inputs_b, inputs_c, steps, log_decay):
    lane_total, length, heads_dev, head_width = values.shape
    state_dim = inputs_b.shape[-1]
    block_total = length // BLOCK

    def blocked(source_array):
        return source_array.reshape((lane_total, block_total, BLOCK) + source_array.shape[2:])

    value_blocks = blocked(values)
    b_rows = blocked(inputs_b)
    c_rows = blocked(inputs_c)
    step_blocks = blocked(steps)
    cumulative = jnp.cumsum(blocked(log_decay), axis=2)
    scores = jnp.einsum("gbtn,gbsn->gbts", c_rows, b_rows, precision=PRECISE)
    gaps = cumulative[:, :, :, None, :] - cumulative[:, :, None, :, :]
    causal = jnp.arange(BLOCK)[:, None] >= jnp.arange(BLOCK)[None, :]
    weights = (
        jnp.exp(jnp.where(causal[:, :, None], gaps, -jnp.inf))
        * scores[..., None]
        * step_blocks[:, :, None, :, :]
    )
    within = jnp.einsum("gbtsh,gbshp->gbthp", weights, value_blocks, precision=PRECISE)
    tail_weight = jnp.exp(cumulative[:, :, -1:, :] - cumulative) * step_blocks
    block_states = jnp.einsum(
        "gbsh,gbsn,gbshp->gbhpn", tail_weight, b_rows, value_blocks, precision=PRECISE
    )
    block_decay = cumulative[:, :, -1, :]

    def advance(state_carry, block_item):
        return (jnp.exp(block_item[0])[..., None, None] * state_carry + block_item[1], state_carry)

    start_state = jnp.zeros((lane_total, heads_dev, head_width, state_dim), jnp.float32)
    final_state, entering = lax.scan(
        advance, start_state, (jnp.moveaxis(block_decay, 1, 0), jnp.moveaxis(block_states, 1, 0))
    )
    entering = jnp.moveaxis(entering, 0, 1)
    across = jnp.exp(cumulative)[..., None] * jnp.einsum(
        "gbtn,gbhpn->gbthp", c_rows, entering, precision=PRECISE
    )
    local_out = (within + across).reshape(values.shape)
    run_decay = jnp.cumsum(log_decay, axis=1)
    return (local_out, run_decay, jnp.sum(block_decay, axis=1), final_state)


def combine_states(earlier, later):
    return (earlier[0] + later[0], jnp.exp(later[0])[..., None, None] * earlier[1] + later[1])


def shards(
    hidden,
    base_ids,
    norm_gain,
    w_gate,
    w_value,
    w_bc,
    w_step,
    conv_value,
    conv_bc,
    step_bias,
    decay_rate,
    skip_gain,
    out_gain,
    w_out,
):
    keep_own = (base_ids != 4).astype(jnp.float32)
    bit_total = lax.axis_size("ctx").bit_length() - 1
    partner = (hidden, base_ids)
    for bit_pos in range(bit_total):
        partner = swapped((partner[0], partner[1]), "ctx", bit_pos)
    other_rows = partner[0][::-1, ::-1]
    other_keep = (partner[1][::-1] != 4).astype(jnp.float32)
    branches = jnp.stack([hidden, other_rows])
    keep_both = jnp.stack([keep_own, other_keep])
    inv_rms = lax.rsqrt(jnp.mean(jnp.square(branches.astype(jnp.float32)), axis=-1) + EPSILON)
    scaled = (branches * norm_gain).astype(jnp.bfloat16)

    def project(weight):
        return (
            jnp.einsum("btd,dk->btk", scaled, weight, preferred_element_type=jnp.float32)
            * inv_rms[..., None]
        )

    gate_in = project(w_gate)
    value_in = project(w_value)
    bc_in = project(w_bc)
    step_in = project(w_step)
    heads_dev = w_step.shape[1]
    inner_dev = w_gate.shape[1]
    head_width = inner_dev // heads_dev
    state_dim = w_bc.shape[1] // 2
    length = hidden.shape[0]
    mixed_in = jnp.concatenate([value_in, bc_in], axis=-1)
    padded = padded_2(mixed_in, (("ctx", 1),), CONV_WIDTH - 1)
    kernel = jnp.concatenate([conv_value, conv_bc], axis=-1)
    forward_mix, backward_mix = convolve(padded, kernel, CONV_WIDTH)
    lane_mix = jax.nn.silu(jnp.concatenate([forward_mix, backward_mix], axis=0))
    keep_lanes = jnp.concatenate([keep_both, keep_both], axis=0)
    values = (lane_mix[..., :inner_dev] * keep_lanes[..., None]).reshape(
        4, length, heads_dev, head_width
    )
    inputs_b = lane_mix[..., inner_dev : inner_dev + state_dim]
    inputs_c = lane_mix[..., inner_dev + state_dim :]
    steps = jax.nn.softplus(step_in + step_bias)
    log_decay = -decay_rate * steps
    steps_lanes = jnp.concatenate([steps, steps], axis=0)
    decay_lanes = jnp.concatenate([log_decay, log_decay], axis=0)
    values = lane_flip(values)
    inputs_b = lane_flip(inputs_b)
    inputs_c = lane_flip(inputs_c)
    local_out, run_decay, device_decay, final_state = local_scan(
        values, inputs_b, inputs_c, lane_flip(steps_lanes), lane_flip(decay_lanes)
    )
    zero_decay = jnp.zeros((2, heads_dev), jnp.float32)
    zero_state = jnp.zeros((2, heads_dev, head_width, state_dim), jnp.float32)
    upward = prefix(
        (device_decay[:2], final_state[:2]), "ctx", combine_states, (zero_decay, zero_state), False
    )
    downward = prefix(
        (device_decay[2:], final_state[2:]), "ctx", combine_states, (zero_decay, zero_state), True
    )
    incoming = jnp.concatenate([upward[1], downward[1]], axis=0)
    chain_part = jnp.exp(run_decay)[..., None] * jnp.einsum(
        "gtn,ghpn->gthp", inputs_c, incoming, precision=PRECISE
    )
    lane_out = lane_flip(local_out + chain_part + skip_gain[:, None] * values)
    summed = lane_out[:2] + lane_out[2:]
    gated = summed * jax.nn.silu(gate_in).reshape(2, length, heads_dev, head_width)
    normed = (
        gated
        * lax.rsqrt(jnp.mean(jnp.square(gated), axis=-1, keepdims=True) + EPSILON)
        * out_gain.reshape(heads_dev, head_width)
    ).astype(jnp.bfloat16)
    term = jnp.einsum(
        "gtk,kd->gtd",
        normed.reshape(2, length, inner_dev),
        w_out,
        preferred_element_type=jnp.float32,
    )
    own_part, other_part = (
        lax.psum_scatter(term[0], "head", scatter_dimension=1, tiled=True),
        lax.psum_scatter(term[1][::-1, ::-1], "head", scatter_dimension=1, tiled=True),
    )
    for bit_pos in range(bit_total):
        other_part = swapped(other_part, "ctx", bit_pos)
    total = own_part + other_part
    return total.astype(jnp.bfloat16)


def solution(mesh):
    return jax.shard_map(
        shards,
        mesh=mesh,
        in_specs=(
            P("ctx", None),
            P("ctx"),
            P(),
            P(None, "head"),
            P(None, "head"),
            P(),
            P(None, "head"),
            P(None, "head"),
            P(),
            P("head"),
            P("head"),
            P("head"),
            P("head"),
            P("head", None),
        ),
        out_specs=P("ctx", "head"),
        check_vma=False,
    )
```

profile of v0, /device:TPU:0, one launch (start us, length us, event | category | flops | bytes accessed | tf_op | source)
XLA Modules:
  0.0 1027.9 jit_solution(16050802928551170397)
XLA Ops:
  7.0 7.0 collective-permute-done
  14.0 2.9 collective-permute-start.1
  16.9 91.0 %collective-permute-done.1 = bf16[512,4096]{1,0:T(8,128)(2,1)} collective-permute-done((bf16[512,4096]{1,0:T(8,128)(2,1)S(1)}, bf16[512,4096]{1,0:T(8,128)(2,1)}, u32[]{:S(2)}, u32[]{:S(2)}) %collective-permute-start.1) | collective-permute-done | bytes 4194336 | tf_op jit(solution)/shard_map/ppermute | solution.py:15
  107.9 2.8 collective-permute-start.2
  114.3 86.0 %collective-permute-done.6 = s32[512]{0:T(512)S(1)} collective-permute-done((s32[512]{0:T(512)S(1)}, s32[512]{0:T(512)S(1)}, u32[]{:S(2)}, u32[]{:S(2)}) %collective-permute-start.6) | collective-permute-done | bytes 2080 | tf_op jit(solution)/shard_map/ppermute | solution.py:15
  203.4 87.8 %collective-permute-done.7 = s32[512]{0:T(512)S(1)} collective-permute-done((s32[512]{0:T(512)S(1)}, s32[512]{0:T(512)S(1)}, u32[]{:S(2)}, u32[]{:S(2)}) %collective-permute-start.7) | collective-permute-done | bytes 2080 | tf_op jit(solution)/shard_map/ppermute | solution.py:15
  291.4 63.3 %rev.27 = bf16[512,4096]{1,0:T(8,128)(2,1)} reverse(bf16[512,4096]{1,0:T(8,128)(2,1)} %collective-permute-done.2), dimensions={0,1} | reverse | bytes 8388608 | tf_op jit(solution)/shard_map/rev | solution.py:133
  354.7 5.7 fusion.7
  363.7 4.6 reduce-window.14
  368.9 13.8 %fusion.37 = f32[2,512,1024]{2,1,0:T(8,128)S(1)} fusion(bf16[4096,1024]{1,0:T(8,128)(2,1)} %param.24, f32[2,512]{1,0:T(2,128)S(1)} %add_rsqrt_fusion.1, f32[4096]{0:T(1024)S(1)} %copy-done.30, bf16[1,512,4096]{2,1,0:T(8,128)(2,1)} %bitcast.168, bf16[1,512,4096]{2,1,0:T(8,128)(2,1)} %bitcast.178), kind=kOutput, calls=%fused_computation.72 | convolution fusion | flops 8607760384 | bytes 20992000 | tf_op jit(solution)/shard_map/btd,dk->btk/dot_general | solution.py:142
  390.3 4.6 maximum_maximum_fusion
  394.9 17.6 %fusion.29 = (f32[2,512,1280]{2,1,0:T(8,128)}, f32[2,512,1280]{2,1,0:T(8,128)}) fusion(f32[2,515,1280]{2,1,0:T(8,128)} %get-tuple-element.249, f32[2,512,256]{2,1,0:T(8,128)S(1)} %fusion.50, f32[2,512,1024]{2,1,0:T(8,128)} %copy-done.8, f32[1280]{0:T(1024)S(1)} %get-tuple-element.206, f32[1280]{0:T(1024)S(1)} %get-tuple-element.207, ...), kind=kLoop, calls=%fused_computation.59 | loop fusion | flops 18350080 | bytes 47206400 | tf_op jit(solution)/shard_map/add | solution.py:53
  412.6 5.9 divide_multiply_fusion
  418.5 4.0 copy-done.6
  423.9 3.9 slice_multiply_fusion
  427.8 4.2 fusion.72
  432.0 5.3 copy.79
  437.3 7.4 rev.29
  444.7 4.8 copy.133
  449.5 7.3 reshape.125
  456.8 7.8 copy.80
  467.2 10.0 fusion.42
  477.2 6.6 while.41
  486.4 4.6 reduce-window.16
  491.2 15.6 %divide_multiply_fusion.1 = f32[2,512,1024]{2,1,0:T(8,128)} fusion(bf16[4096,1024]{1,0:T(8,128)(2,1)} %param.23, f32[2,512]{1,0:T(2,128)S(1)} %add_rsqrt_fusion.1, f32[4096]{0:T(1024)} %param.22, bf16[1,512,4096]{2,1,0:T(8,128)(2,1)} %bitcast.169, bf16[1,512,4096]{2,1,0:T(8,128)(2,1)} %bitcast.179), kind=kOutput, calls=%fused_computation.70 | convolution fusion | flops 8611954688 | bytes 20992000 | tf_op jit(solution)/shard_map/btd,dk->btk/dot_general | solution.py:142
  506.9 5.5 copy.96
  512.3 14.9 %all-gather.4 = f32[8,2,16]{2,1,0:T(2,128)S(1)} all-gather(f32[1,2,16]{2,1,0:T(2,128)S(1)} %get-tuple-element.259), channel_id=2, replica_groups=mesh['ctx'=8,'head'=4] {'ctx'}, dimensions={0}, use_global_device_ids=true | all-gather | bytes 1152 | tf_op jit(solution)/shard_map/all_gather | solution.py:35
  527.2 8.9 all-gather.5
  536.2 5.6 copy.95
  544.1 6.8 fusion.34
  550.9 38.4 %fusion.19 = f32[4,2,16,8,8,256]{5,4,3,2,1,0:T(8,128)S(1)} fusion(f32[4,2,256,16,64]{2,4,3,1,0:T(8,128)S(1)} %fusion.34, f32[4,2,256,16]{2,3,1,0:T(8,128)S(1)} %bitcast.190, f32[4,2,256,256]{3,2,1,0:T(8,128)S(1)} %fusion.74, f32[4,2,256,16]{2,3,1,0:T(8,128)S(1)} %copy-done.25, pred[256,256]{1,0:T(8,128)(4,1)S(1)} %iota_compare_fusion, ...), kind=kOutput, calls=%fused_computation.41 | convolution fusion | flops 6482296832 | bytes 27721728 | tf_op jit(solution)/shard_map/gbtsh,gbshp->gbthp/dot_general | solution.py:85
  589.3 4.3 copy.115
  593.7 59.7 %all-gather.11.cloned.1.call-done = f32[16,16,64,128]{3,2,1,0:T(8,128)} async-done(((f32[2,16,64,128]{3,2,1,0:T(8,128)}), f32[16,16,64,128]{3,2,1,0:T(8,128)}) %all-gather.11.cloned.1.call-update) | async-done | bytes 8388624 | tf_op jit(solution)/shard_map/all_gather | solution.py:35
  653.5 10.6 %while.40 = (s32[]{:T(128)}, f32[2,16,64,128]{3,2,1,0:T(8,128)S(1)}, s32[]{:T(128)}, f32[8,2,16]{2,1,0:T(2,128)S(1)}, f32[8,2,16,64,128]{4,3,2,1,0:T(8,128)}, /*index=5*/s32[]{:T(128)}, s32[]{:T(128)}, s32[]{:T(128)}, s32[]{:T(128)}) while((s32[]{:T(128)}, f32[2,16,64,128]{3,2,1,0:T(8,128)S(1)}, s32[]{:T(128)}, f32[8,2,16]{2,1,0:T(2,128)S(1)}, ...), condition=%wide.region_11.12_spmd, body=%wide.region_10.11_spmd.sunk | while | flops 524294 | bytes 3146259 | solution.py:44
  664.1 13.0 %fusion.14 = f32[4,512,16,64]{1,3,2,0:T(8,128)S(1)} fusion(f32[2,512,16,64]{1,3,2,0:T(8,128)} %rev.29, f32[2,512,16,64]{1,3,2,0:T(8,128)} %bitcast.172, f32[4,512,16,64]{1,3,2,0:T(8,128)} %bitcast.163, f32[16]{0:T(128)S(1)} %copy-done.28, f32[4,512,16]{1,2,0:T(8,128)S(1)} %bitcast_bitcast_fusion, f32[2,16,64,128]{3,2,1,0:T(8,128)S(1)} %get-tuple-element.164, ...), kind=kOutput, calls=%fused_computation.35 | convolution fusion | flops 3232497664 | bytes 28442688 | tf_op jit(solution)/shard_map/gtn,ghpn->gthp/dot_general | solution.py:185
  677.1 3.3 copy-done.3
  682.8 7.4 rev.34
  690.2 6.6 multiply_reduce_fusion
  698.4 3.3 multiply_convert_fusion
  701.7 11.7 %fusion.15 = f32[2,512,4096]{2,1,0:T(8,128)S(1)} fusion(bf16[2,512,1024]{1,2,0:T(8,128)(2,1)S(1)} %bitcast.184, bf16[1024,4096]{1,0:T(8,128)(2,1)} %param.33), kind=kOutput, calls=%fused_computation.36 | convolution fusion | flops 8589934592 | bytes 27262976 | tf_op jit(solution)/shard_map/gtk,kd->gtd/dot_general | solution.py:196
  713.4 6.4 slice_bitcast_fusion
  719.8 67.7 %rev.35 = f32[512,4096]{1,0:T(8,128)} reverse(f32[512,4096]{1,0:T(8,128)} %get-tuple-element.239), dimensions={0,1} | reverse | bytes 16777216 | tf_op jit(solution)/shard_map/rev | solution.py:204
  788.1 84.2 %reduce-scatter.5.cloned.1.call-done = f32[512,1024]{1,0:T(8,128)} async-done(((f32[512,4096]{1,0:T(8,128)}), f32[512,1024]{1,0:T(8,128)}) %reduce-scatter.5.cloned.1.call-update) | async-done | bytes 2097168 | tf_op jit(solution)/shard_map/reduce_scatter | solution.py:204
  872.3 4.4 collective-permute-done.8
  878.1 46.3 %collective-permute-done.9 = f32[512,1024]{1,0:T(8,128)} collective-permute-done((f32[512,1024]{1,0:T(8,128)S(1)}, f32[512,1024]{1,0:T(8,128)}, u32[]{:S(2)}, u32[]{:S(2)}) %collective-permute-start.9) | collective-permute-done | bytes 2097184 | tf_op jit(solution)/shard_map/ppermute | solution.py:15
  926.8 35.1 %reduce-scatter.3.cloned.1.call-done = f32[512,1024]{1,0:T(8,128)} async-done(((f32[512,4096]{1,0:T(8,128)}), f32[512,1024]{1,0:T(8,128)}) %reduce-scatter.3.cloned.1.call-update) | async-done | bytes 2097168 | tf_op jit(solution)/shard_map/reduce_scatter | solution.py:203
  961.9 55.5 %collective-permute-done.10 = f32[512,1024]{1,0:T(8,128)} collective-permute-done((f32[512,1024]{1,0:T(8,128)}, f32[512,1024]{1,0:T(8,128)}, u32[]{:S(2)}, u32[]{:S(2)}) %collective-permute-start.10) | collective-permute-done | bytes 2097184 | tf_op jit(solution)/shard_map/ppermute | solution.py:15
  1017.5 3.5 add_convert_fusion
  (156 shorter events, 53.3 us)
Async XLA Ops:
  6.5 376.2 %copy-start = (bf16[4096,256]{1,0:T(8,128)(2,1)S(1)}, bf16[4096,256]{1,0:T(8,128)(2,1)}, u32[]{:S(2)}) copy-start(bf16[4096,256]{1,0:T(8,128)(2,1)} %param.25) | copy-start | bytes 6291460
  6.5 587.1 %all-gather.9.cloned.1.call-start = ((), (), s32[]{:S(2)}) async-start(), calls=%async_computation.4 | async-start | bytes 9437184 | tf_op jit(solution)/shard_map/all_gather | solution.py:35
  6.5 7.4 collective-permute-start
  14.0 93.9 %collective-permute-start.1 = (bf16[512,4096]{1,0:T(8,128)(2,1)S(1)}, bf16[512,4096]{1,0:T(8,128)(2,1)}, u32[]{:S(2)}, u32[]{:S(2)}) collective-permute-start(bf16[512,4096]{1,0:T(8,128)(2,1)S(1)} %collective-permute-done), channel_id=1, source_target_pairs={{0,8},{4,12},{8,0},{12,4},{16,24},{20,28},{24,16},{28,20},{1,9},{5... | collective-permute-start | bytes 12582920 | tf_op jit(solution)/shard_map/ppermute | solution.py:15
  107.9 183.4 %collective-permute-start.2 = (bf16[512,4096]{1,0:T(8,128)(2,1)}, bf16[512,4096]{1,0:T(8,128)(2,1)}, u32[]{:S(2)}, u32[]{:S(2)}) collective-permute-start(bf16[512,4096]{1,0:T(8,128)(2,1)} %collective-permute-done.1), channel_id=1, source_target_pairs={{0,16},{4,20},{8,24},{12,28},{16,0},{20,4},{24,8},{28,12},{1,17},{... | collective-permute-start | bytes 12582920 | tf_op jit(solution)/shard_map/ppermute | solution.py:15
  110.7 1.4 collective-permute-start.5
  112.1 88.3 %collective-permute-start.6 = (s32[512]{0:T(512)S(1)}, s32[512]{0:T(512)S(1)}, u32[]{:S(2)}, u32[]{:S(2)}) collective-permute-start(s32[512]{0:T(512)S(1)} %collective-permute-done.5), channel_id=1, source_target_pairs={{0,8},{4,12},{8,0},{12,4},{16,24},{20,28},{24,16},{28,20},{1,9},{5... | collective-permute-start | bytes 6152 | tf_op jit(solution)/shard_map/ppermute | solution.py:15
  200.4 90.8 %collective-permute-start.7 = (s32[512]{0:T(512)S(1)}, s32[512]{0:T(512)S(1)}, u32[]{:S(2)}, u32[]{:S(2)}) collective-permute-start(s32[512]{0:T(512)S(1)} %collective-permute-done.6), channel_id=1, source_target_pairs={{0,16},{4,20},{8,24},{12,28},{16,0},{20,4},{24,8},{28,12},{1,17},{... | collective-permute-start | bytes 6152 | tf_op jit(solution)/shard_map/ppermute | solution.py:15
  291.3 69.0 %copy-start.29 = (bf16[4096,16]{0,1:T(8,128)(2,1)S(1)}, bf16[4096,16]{0,1:T(8,128)(2,1)}, u32[]{:S(2)}) copy-start(bf16[4096,16]{0,1:T(8,128)(2,1)} %param.26) | copy-start | bytes 393220
  291.3 69.0 %copy-start.30 = (f32[4096]{0:T(1024)S(1)}, f32[4096]{0:T(1024)}, u32[]{:S(2)}) copy-start(f32[4096]{0:T(1024)} %param.22) | copy-start | bytes 49156
  354.7 5.7 copy-start.12
  354.7 6.0 copy-start.21
  354.7 6.0 copy-start.31
  368.6 14.0 %copy-start.24 = (f32[4,2,256,16]{2,3,1,0:T(8,128)}, f32[4,2,256,16]{2,3,1,0:T(8,128)S(1)}, u32[]{:S(2)}) copy-start(f32[4,2,256,16]{2,3,1,0:T(8,128)S(1)} %bitcast_bitcast_fusion.1) | copy-start | bytes 393220
  368.8 13.9 %copy-start.13 = (bf16[512,4096]{1,0:T(8,128)(2,1)S(1)}, bf16[512,4096]{1,0:T(8,128)(2,1)}, u32[]{:S(2)}) copy-start(bf16[512,4096]{1,0:T(8,128)(2,1)} %rev.27) | copy-start | bytes 12582916
  368.9 13.9 %copy-start.22 = (bf16[512,4096]{1,0:T(8,128)(2,1)S(1)}, bf16[512,4096]{1,0:T(8,128)(2,1)}, u32[]{:S(2)}) copy-start(bf16[512,4096]{1,0:T(8,128)(2,1)} %param.20) | copy-start | bytes 12582916
  382.7 7.6 copy-start.8
  385.1 3.6 collective-permute-start.3
  386.4 3.9 collective-permute-start.4
  418.5 4.0 copy-start.6
  423.4 41.2 %copy-start.19 = (f32[2,512,128]{2,1,0:T(8,128)}, f32[2,512,128]{2,1,0:T(8,128)S(1)}, u32[]{:S(2)}) copy-start(f32[2,512,128]{2,1,0:T(8,128)S(1)} %get-tuple-element.244) | copy-start | bytes 1572868
  423.7 41.0 %copy-start.17 = (f32[2,512,128]{2,1,0:T(8,128)}, f32[2,512,128]{2,1,0:T(8,128)S(1)}, u32[]{:S(2)}) copy-start(f32[2,512,128]{2,1,0:T(8,128)S(1)} %rev.31) | copy-start | bytes 1572868
  456.8 7.8 copy-start.23
  464.6 2.6 copy-start.9
  464.8 12.4 %copy-start.15 = (f32[4,512,128]{2,1,0:T(8,128)}, f32[4,512,128]{2,1,0:T(8,128)S(1)}, u32[]{:S(2)}) copy-start(f32[4,512,128]{2,1,0:T(8,128)S(1)} %get-tuple-element.265) | copy-start | bytes 3145732
  467.2 10.0 copy-start.2
  477.2 2.9 copy-start.5
  480.5 2.9 copy-start.5
  483.8 2.4 copy-start.27
  485.4 167.9 %all-gather.11.cloned.1.call-start = ((), (), s32[]{:S(2)}) async-start(), calls=%async_computation.5 | async-start | bytes 9437184 | tf_op jit(solution)/shard_map/all_gather | solution.py:35
  486.2 386.1 %reduce-scatter.5.cloned.1.call-start = ((), (), s32[]{:S(2)}) async-start(), calls=%async_computation.3 | async-start | bytes 10485760 | tf_op jit(solution)/shard_map/reduce_scatter | solution.py:204
  512.3 29.5 %copy-start.16 = (f32[4,512,128]{2,1,0:T(8,128)S(1)}, f32[4,512,128]{2,1,0:T(8,128)}, u32[]{:S(2)}) copy-start(f32[4,512,128]{2,1,0:T(8,128)} %copy-done.15) | copy-start | bytes 3145732
  541.8 2.3 copy-start.14
  544.1 6.8 copy-start.10
  544.1 6.8 copy-start.11
  544.1 6.8 copy-start.25
  544.1 6.8 copy-start.26
  653.5 10.6 %copy-start.18 = (f32[2,512,128]{2,1,0:T(8,128)S(1)}, f32[2,512,128]{2,1,0:T(8,128)}, u32[]{:S(2)}) copy-start(f32[2,512,128]{2,1,0:T(8,128)} %copy-done.17) | copy-start | bytes 1572868
  653.5 10.6 %copy-start.20 = (f32[2,512,128]{2,1,0:T(8,128)S(1)}, f32[2,512,128]{2,1,0:T(8,128)}, u32[]{:S(2)}) copy-start(f32[2,512,128]{2,1,0:T(8,128)} %copy-done.19) | copy-start | bytes 1572868
  653.5 10.6 %copy-start.28 = (f32[16]{0:T(128)S(1)}, f32[16]{0:T(128)}, u32[]{:S(2)}) copy-start(f32[16]{0:T(128)} %param.31) | copy-start | bytes 196
  677.1 3.3 copy-start.3
  690.2 7.0 copy-start.4
  690.2 8.2 copy-start.7
  787.5 174.4 %reduce-scatter.3.cloned.1.call-start = ((), (), s32[]{:S(2)}) async-start(), calls=%async_computation.2 | async-start | bytes 10485760 | tf_op jit(solution)/shard_map/reduce_scatter | solution.py:203
  787.6 233.4 %copy-start.1 = (bf16[4096,256]{1,0:T(8,128)(2,1)S(1)}, bf16[4096,256]{1,0:T(8,128)(2,1)}, u32[]{:S(2)}) copy-start(bf16[4096,256]{1,0:T(8,128)(2,1)} %param.25) | copy-start | bytes 6291460
  872.3 4.4 collective-permute-start.8
  876.7 47.8 %collective-permute-start.9 = (f32[512,1024]{1,0:T(8,128)S(1)}, f32[512,1024]{1,0:T(8,128)}, u32[]{:S(2)}, u32[]{:S(2)}) collective-permute-start(f32[512,1024]{1,0:T(8,128)S(1)} %collective-permute-done.8), channel_id=1, source_target_pairs={{0,8},{4,12},{8,0},{12,4},{16,24},{20,28},{24,16},{28,20},{1,9},{5... | collective-permute-start | bytes 6291464 | tf_op jit(solution)/shard_map/ppermute | solution.py:15
  924.5 93.0 %collective-permute-start.10 = (f32[512,1024]{1,0:T(8,128)}, f32[512,1024]{1,0:T(8,128)}, u32[]{:S(2)}, u32[]{:S(2)}) collective-permute-start(f32[512,1024]{1,0:T(8,128)} %collective-permute-done.9), channel_id=1, source_target_pairs={{0,16},{4,20},{8,24},{12,28},{16,0},{20,4},{24,8},{28,12},{1,17},{... | collective-permute-start | bytes 6291464 | tf_op jit(solution)/shard_map/ppermute | solution.py:15
Sparse Core Ops, SparseCore 0:
  485.6 85.5 all-gather.8
  572.7 80.5 all-gather.10
  787.6 84.6 reduce-scatter.4
  875.5 86.3 reduce-scatter.2
where the time goes:
time: 1050 us; the launch traced here: 1030 us
  waiting for transfers between devices  560 us (53%)
  local copies, waits for them, and re-layouts  220 us (21%)
  matrix products  116 us (11%)
  other arithmetic  77.2 us (7%)
  blocking collectives  23.8 us (2%)
  starting transfers between devices  16.8 us (2%)
  between operations  14.2 us (1%)
    ppermute x9, waiting for transfers between devices, swapped(): lax.ppermute(array, axis, [(i, i ^ 1 << stride) for i in range(lax.axis_s...  378 us
    reduce_scatter x1, waiting for transfers between devices, shards(): lax.psum_scatter(term[1][::-1, ::-1], 'head', scatter_dimension=1, tiled=...  84.2 us
    rev x1, local copies, waits for them, and re-layouts, shards(): term[1][::-1, ::-1]  67.7 us
    rev x1, local copies, waits for them, and re-layouts, shards(): other_rows = partner[0][::-1, ::-1]  63.3 us
    all_gather x2, waiting for transfers between devices, prefix(): gathered = jax.tree.map(lambda a: lax.all_gather(a, axis), part)  59.7 us
    dot_general x1, matrix products, local_scan(): jnp.einsum('gbtsh,gbshp->gbthp', weights, value_blocks, precision=PRECISE)  38.4 us
    reduce_scatter x1, waiting for transfers between devices, shards(): lax.psum_scatter(term[0], 'head', scatter_dimension=1, tiled=True)  35.1 us
    dot_general x4, matrix products, project(): jnp.einsum('btd,dk->btk', scaled, weight, preferred_element_type=jnp.floa...  34.1 us
  transfers between devices with their start and end apart: 15, of which 11 were waited for; matrix products, arithmetic and copies ran while one was open for 8% of the time, Pallas kernels for 0%

commit v1 on v0

v1 whole, which is shorter than its diff:
```python
import functools

import jax
import jax.numpy as jnp
from jax import lax
from jax.experimental import pallas as pl
from jax.experimental.pallas import tpu as pltpu
from jax.sharding import PartitionSpec as P

EPSILON = 1e-05
PRECISE = lax.Precision.HIGHEST
F32 = jnp.float32
BF16 = jnp.bfloat16
COLS = 256
ROWS = 128
HALO = 8
VMEM_LIMIT = 56 * 1024 * 1024


def params(dims):
    return pltpu.CompilerParams(
        vmem_limit_bytes=VMEM_LIMIT, dimension_semantics=("arbitrary",) * dims
    )


def anti_identity(size):
    row = lax.broadcasted_iota(jnp.int32, (size, size), 0)
    col = lax.broadcasted_iota(jnp.int32, (size, size), 1)
    return (row + col == size - 1).astype(F32).astype(BF16)


def matmul(a, b):
    return jnp.dot(a, b, preferred_element_type=F32)


def spread(per_head, width):
    heads = per_head.shape[1]
    high = per_head.astype(BF16)
    low = (per_head - high.astype(F32)).astype(BF16)
    row = lax.broadcasted_iota(jnp.int32, (heads, heads * width), 0)
    col = lax.broadcasted_iota(jnp.int32, (heads, heads * width), 1)
    pick = ((col >= row * width) & (col < (row + 1) * width)).astype(F32).astype(BF16)
    return matmul(high, pick) + matmul(low, pick)


def silu(x):
    return x * (1.0 / (1.0 + jnp.exp(-x)))


def prepare_kernel(own_ref, mirror_ref, gain_ref, scaled_ref, squares_ref):
    own = own_ref[...].astype(F32)
    gain = gain_ref[...]
    scaled_ref[0] = (own * gain).astype(BF16)
    flipped = matmul(mirror_ref[...], anti_identity(COLS))
    scaled_ref[1] = (flipped * gain).astype(BF16)

    @pl.when(pl.program_id(0) == 0)
    def _():
        squares_ref[...] = jnp.zeros_like(squares_ref)

    square = own * own
    squares_ref[...] += square[:, :128] + square[:, 128:]


def prepare(hidden, gain):
    length, depth = hidden.shape
    count = depth // COLS
    return pl.pallas_call(
        prepare_kernel,
        grid=(count,),
        in_specs=[
            pl.BlockSpec((length, COLS), lambda j: (0, j)),
            pl.BlockSpec((length, COLS), lambda j: (0, count - 1 - j)),
            pl.BlockSpec((1, COLS), lambda j: (0, j)),
        ],
        out_specs=[
            pl.BlockSpec((2, length, COLS), lambda j: (0, 0, j)),
            pl.BlockSpec((length, 128), lambda j: (0, 0)),
        ],
        out_shape=[
            jax.ShapeDtypeStruct((2, length, depth), BF16),
            jax.ShapeDtypeStruct((length, 128), F32),
        ],
        compiler_params=params(1),
        name="prepare",
    )(hidden, hidden, gain[None])


def convolve(out, ext, main_ref, before_ref, after_ref, taps_ref):
    length = main_ref.shape[1]
    ext[0:HALO] = before_ref[0]
    ext[HALO : HALO + length] = main_ref[0]
    ext[HALO + length :] = after_ref[0]
    taps = [taps_ref[k : k + 1, :] for k in range(4)]
    step = 64
    for start in range(0, length, step):
        rows = [ext[start + HALO - 3 + k : start + HALO - 3 + k + step] for k in range(7)]
        forward = taps[0] * rows[0]
        backward = taps[0] * rows[6]
        for k in range(1, 4):
            forward = forward + taps[k] * rows[k]
            backward = backward + taps[k] * rows[6 - k]
        out(start, step, silu(forward), silu(backward))


def mix_kernel(
    v_ref, bc_ref, before_v, before_bc, after_v, after_bc, taps_v, taps_bc, aux_ref, keep_ref,
    x_ref, bco_ref, bt_ref, s_ref, ext,
):
    c = pl.program_id(1)
    length = v_ref.shape[1]

    @pl.when(c == 0)
    def _():
        def out(start, step, forward, backward):
            bco_ref[0, 0, start : start + step] = forward.astype(BF16)
            bco_ref[0, 1, start : start + step] = backward.astype(BF16)

        convolve(out, ext, bc_ref, before_bc, after_bc, taps_bc)
        state = bt_ref.shape[2]
        for d in range(2):
            bt_ref[0, d] = bco_ref[0, d, :, :state].astype(F32).T.astype(BF16)

    @pl.when(c > 0)
    def _():
        def out(start, step, forward, backward):
            keep = keep_ref[start : start + step]
            x_ref[0, 0, start : start + step] = (forward * keep).astype(BF16)
            x_ref[0, 1, start : start + step] = (backward * keep).astype(BF16)

        convolve(out, ext, v_ref, before_v, after_v, taps_v)
        heads = aux_ref.shape[3] // 3
        aux = aux_ref[0, 0]
        steps = aux[:, 2 * heads :]
        for d in range(2):
            cum = aux[:, d * heads : (d + 1) * heads]
            total = cum[length - 1 :] if d == 0 else cum[:1]
            weight = spread(jnp.exp(total - cum) * steps, COLS // heads)
            s_ref[0, d] = matmul(bt_ref[0, d], (x_ref[0, d].astype(F32) * weight).astype(BF16))


def mix(value_in, bc_in, before, after, conv_value, conv_bc, aux, keep):
    _, length, inner = value_in.shape
    pair = bc_in.shape[2]
    state = pair // 2
    chunks = inner // COLS
    before_v, before_bc = before[..., :inner], before[..., inner:]
    after_v, after_bc = after[..., :inner], after[..., inner:]

    def at(c):
        return jnp.maximum(c - 1, 0)

    return pl.pallas_call(
        mix_kernel,
        grid=(2, chunks + 1),
        in_specs=[
            pl.BlockSpec((1, length, COLS), lambda b, c: (b, 0, at(c))),
            pl.BlockSpec((1, length, pair), lambda b, c: (b, 0, 0)),
            pl.BlockSpec((1, HALO, COLS), lambda b, c: (b, 0, at(c))),
            pl.BlockSpec((1, HALO, pair), lambda b, c: (b, 0, 0)),
            pl.BlockSpec((1, HALO, COLS), lambda b, c: (b, 0, at(c))),
            pl.BlockSpec((1, HALO, pair), lambda b, c: (b, 0, 0)),
            pl.BlockSpec((4, COLS), lambda b, c: (0, at(c))),
            pl.BlockSpec((4, pair), lambda b, c: (0, 0)),
            pl.BlockSpec((1, 1) + aux.shape[2:], lambda b, c: (b, at(c), 0, 0)),
            pl.BlockSpec((length, 1), lambda b, c: (0, 0)),
        ],
        out_specs=[
            pl.BlockSpec((1, 2, length, COLS), lambda b, c: (b, 0, 0, at(c))),
            pl.BlockSpec((1, 2, length, pair), lambda b, c: (b, 0, 0, 0)),
            pl.BlockSpec((1, 2, state, length), lambda b, c: (b, 0, 0, 0)),
            pl.BlockSpec((1, 2, state, COLS), lambda b, c: (b, 0, 0, at(c))),
        ],
        out_shape=[
            jax.ShapeDtypeStruct((2, 2, length, inner), BF16),
            jax.ShapeDtypeStruct((2, 2, length, pair), BF16),
            jax.ShapeDtypeStruct((2, 2, state, length), BF16),
            jax.ShapeDtypeStruct((2, 2, state, inner), F32),
        ],
        scratch_shapes=[pltpu.VMEM((length + 2 * HALO, COLS), F32)],
        compiler_params=params(2),
        cost_estimate=pl.CostEstimate(
            flops=2 * 4 * length * state * inner,
            bytes_accessed=14 * 2 * length * inner,
            transcendentals=4 * length * inner,
        ),
        name="mix",
    )(value_in, bc_in, before_v, before_bc, after_v, after_bc, conv_value, conv_bc, aux, keep)


def scan_kernel(x_ref, bc_ref, bt_ref, aux_ref, row_ref, skip_ref, y_ref):
    length = x_ref.shape[2]
    state = bt_ref.shape[2]
    heads = aux_ref.shape[3] // 3
    width = COLS // heads
    row = lax.broadcasted_iota(jnp.int32, (ROWS, ROWS), 0)
    col = lax.broadcasted_iota(jnp.int32, (ROWS, ROWS), 1)
    left = (lax.broadcasted_iota(jnp.int32, (1, 2 * width), 1) < width).astype(F32).astype(BF16)
    right = (1.0 - left.astype(F32)).astype(BF16)
    blocks = length // ROWS
    for d in range(2):
        carried = jnp.zeros((state, COLS), F32)
        reach = (row >= col) if d == 0 else (row <= col)
        order = range(blocks) if d == 0 else range(blocks - 1, -1, -1)
        for lap, i in enumerate(order):
            own = slice(i * ROWS, (i + 1) * ROWS)
            aux = aux_ref[0, 0, own]
            cum = aux[:, d * heads : (d + 1) * heads]
            steps = aux[:, 2 * heads :]
            x = x_ref[0, d, own].astype(F32)
            xd = x * spread(steps, width)
            xd16 = xd.astype(BF16)
            c_rows = bc_ref[0, d, own, state:]
            scores = lax.dot_general(
                c_rows, bc_ref[0, d, own, :state], (((1,), (1,)), ((), ())),
                preferred_element_type=F32,
            )
            scores = jnp.where(reach, scores, 0.0)
            parts = []
            for p in range(heads // 2):
                weights = []
                for h in (2 * p, 2 * p + 1):
                    line = row_ref[0, 0, d * heads + h : d * heads + h + 1, own]
                    gap = jnp.minimum(cum[:, h : h + 1] - line, 0.0)
                    weights.append((jnp.exp(gap) * scores).astype(BF16))
                both = xd16[:, 2 * p * width : 2 * (p + 1) * width]
                stacked = jnp.concatenate([both * left, both * right], axis=0)
                parts.append(matmul(jnp.concatenate(weights, axis=1), stacked))
            local = jnp.concatenate(parts, axis=1)
            if lap > 0:
                entry = (i * ROWS - 1) if d == 0 else (i + 1) * ROWS
                base = aux_ref[0, 0, entry : entry + 1, d * heads : (d + 1) * heads]
                local = local + spread(jnp.exp(cum - base), width) * matmul(
                    c_rows, carried.astype(BF16)
                )
            else:
                base = jnp.zeros((1, heads), F32)
            local = local + skip_ref[...] * x
            if d == 0:
                y_ref[0, own] = local
            else:
                y_ref[0, own] += local
            if lap < blocks - 1:
                last = cum[ROWS - 1 :] if d == 0 else cum[:1]
                tail = spread(jnp.exp(last - cum), width)
                fresh = matmul(bt_ref[0, d, :, own], (xd * tail).astype(BF16))
                if lap > 0:
                    decay = spread(jnp.broadcast_to(jnp.exp(last - base), (8, heads)), width)
                    carried = decay[:1] * carried + fresh
                else:
                    carried = fresh


def scan_local(x, bc, bt, aux, rows, skip):
    _, _, length, inner = x.shape
    pair = bc.shape[3]
    state = pair // 2
    chunks = inner // COLS
    return pl.pallas_call(
        scan_kernel,
        grid=(2, chunks),
        in_specs=[
            pl.BlockSpec((1, 2, length, COLS), lambda b, c: (b, 0, 0, c)),
            pl.BlockSpec((1, 2, length, pair), lambda b, c: (b, 0, 0, 0)),
            pl.BlockSpec((1, 2, state, length), lambda b, c: (b, 0, 0, 0)),
            pl.BlockSpec((1, 1) + aux.shape[2:], lambda b, c: (b, c, 0, 0)),
            pl.BlockSpec((1, 1) + rows.shape[2:], lambda b, c: (b, c, 0, 0)),
            pl.BlockSpec((1, COLS), lambda b, c: (0, c)),
        ],
        out_specs=pl.BlockSpec((1, length, COLS), lambda b, c: (b, 0, c)),
        out_shape=jax.ShapeDtypeStruct((2, length, inner), F32),
        compiler_params=params(2),
        cost_estimate=pl.CostEstimate(
            flops=2 * 64 * length * ROWS * inner,
            bytes_accessed=20 * length * inner,
            transcendentals=0,
        ),
        name="scan_local",
    )(x, bc, bt, aux, rows, skip)


def finish_kernel(y_ref, bc_ref, s_ref, aux_ref, gate_ref, gain_ref, out_ref):
    state = s_ref.shape[2]
    heads = aux_ref.shape[3] // 3
    width = COLS // heads
    row = lax.broadcasted_iota(jnp.int32, (COLS, COLS), 0)
    col = lax.broadcasted_iota(jnp.int32, (COLS, COLS), 1)
    same = None
    for h in range(heads):
        low, high = h * width, (h + 1) * width
        square = (row >= low) & (row < high) & (col >= low) & (col < high)
        same = square if same is None else same | square
    same = same.astype(F32).astype(BF16)
    length = y_ref.shape[1]
    for start in range(0, length, ROWS):
        own = slice(start, start + ROWS)
        aux = aux_ref[0, 0, own]
        y = y_ref[0, own]
        for d in range(2):
            grown = spread(jnp.exp(aux[:, d * heads : (d + 1) * heads]), width)
            y = y + grown * matmul(bc_ref[0, d, own, state:], s_ref[0, d])
        gated = y * silu(gate_ref[0, own])
        mean = matmul((gated * gated).astype(BF16), same) * (1.0 / width)
        out_ref[0, own] = (gated * lax.rsqrt(mean + EPSILON) * gain_ref[...]).astype(BF16)


def finish(y, bc, entering, aux, gate_in, gain):
    _, length, inner = y.shape
    pair = bc.shape[3]
    chunks = inner // COLS
    return pl.pallas_call(
        finish_kernel,
        grid=(2, chunks),
        in_specs=[
            pl.BlockSpec((1, length, COLS), lambda b, c: (b, 0, c)),
            pl.BlockSpec((1, 2, length, pair), lambda b, c: (b, 0, 0, 0)),
            pl.BlockSpec((1, 2, pair // 2, COLS), lambda b, c: (b, 0, 0, c)),
            pl.BlockSpec((1, 1) + aux.shape[2:], lambda b, c: (b, c, 0, 0)),
            pl.BlockSpec((1, length, COLS), lambda b, c: (b, 0, c)),
            pl.BlockSpec((1, COLS), lambda b, c: (0, c)),
        ],
        out_specs=pl.BlockSpec((1, length, COLS), lambda b, c: (b, 0, c)),
        out_shape=jax.ShapeDtypeStruct((2, length, inner), BF16),
        compiler_params=params(2),
        name="finish",
    )(y, bc, entering, aux, gate_in, gain)


def project_out_kernel(normed_ref, own_ref, mirror_ref, out_ref):
    flipped = matmul(mirror_ref[...], anti_identity(COLS)).astype(BF16)
    out_ref[...] = (
        matmul(normed_ref[0], own_ref[...]) + matmul(normed_ref[1], flipped)
    ).astype(BF16)


def project_out(normed, w_out):
    _, length, inner = normed.shape
    depth = w_out.shape[1]
    count = depth // COLS
    return pl.pallas_call(
        project_out_kernel,
        grid=(count,),
        in_specs=[
            pl.BlockSpec((2, length, inner), lambda j: (0, 0, 0)),
            pl.BlockSpec((inner, COLS), lambda j: (0, j)),
            pl.BlockSpec((inner, COLS), lambda j: (0, count - 1 - j)),
        ],
        out_specs=pl.BlockSpec((length, COLS), lambda j: (0, j)),
        out_shape=jax.ShapeDtypeStruct((length, depth), BF16),
        compiler_params=params(1),
        name="project_out",
    )(normed, w_out, w_out)


def enter_states(local, log_total, width):
    size = lax.axis_size("ctx")
    odd = lax.axis_index("ctx") % 2 == 1
    swap = [(i, i ^ 1) for i in range(size)]
    ahead = [(i, i + 2) for i in range(1, size - 2, 2)] + [(i, i - 2) for i in range(2, size, 2)]
    decay = jnp.repeat(jnp.exp(log_total), width, axis=-1)[:, None, :]
    other_decay = jnp.repeat(
        jnp.exp(lax.ppermute(log_total, "ctx", swap)), width, axis=-1
    )[:, None, :]
    chip_decay = decay * other_decay
    forward, backward = local[:, 0], local[:, 1]
    received = lax.ppermute(jnp.where(odd, backward, forward).astype(BF16), "ctx", swap).astype(F32)
    chip = decay * received + jnp.where(odd, forward, backward)
    entering = lax.ppermute(chip.astype(BF16), "ctx", ahead)
    for _ in range(size // 2 - 2):
        entering = lax.ppermute(
            (chip + chip_decay * entering.astype(F32)).astype(BF16), "ctx", ahead
        )
    crossed = lax.ppermute(entering, "ctx", swap)
    own = (other_decay * entering.astype(F32) + received).astype(BF16)
    return jnp.stack([jnp.where(odd, own, crossed), jnp.where(odd, crossed, own)], axis=1)


def shards(
    hidden, base_ids, norm_gain, w_gate, w_value, w_bc, w_step, conv_value, conv_bc,
    step_bias, decay_rate, skip_gain, out_gain, w_out,
):
    keep = (base_ids != 4).astype(F32)[:, None]
    length, depth = hidden.shape
    inner = w_gate.shape[1]
    heads = w_step.shape[1]
    width = inner // heads
    chunks = inner // COLS
    per = COLS // width
    scaled, squares = prepare(hidden, norm_gain)
    inv_rms = lax.rsqrt(jnp.sum(squares, axis=-1) / depth + EPSILON)[:, None]

    def project(weight):
        return (
            jnp.einsum("btd,dk->btk", scaled, weight, preferred_element_type=F32) * inv_rms
        )

    bc_in = project(w_bc)
    step_in = project(w_step)
    value_in = project(w_value)
    size = lax.axis_size("ctx")
    up = [(i, i + 1) for i in range(size - 1)]
    down = [(i + 1, i) for i in range(size - 1)]
    tail = jnp.concatenate([value_in[:, length - HALO :], bc_in[:, length - HALO :]], axis=-1)
    head = jnp.concatenate([value_in[:, :HALO], bc_in[:, :HALO]], axis=-1)
    before = lax.ppermute(tail, "ctx", up)
    after = lax.ppermute(head, "ctx", down)
    gate_in = project(w_gate)

    steps = jax.nn.softplus(step_in + step_bias)
    log_decay = -decay_rate * steps
    lower = jnp.tril(jnp.ones((length, length), F32))
    triangles = jnp.stack([lower, lower.T])
    cum = jnp.einsum("dts,bsh->bdth", triangles, log_decay, precision=PRECISE)
    log_total = cum[:, 0, -1]
    packed = jnp.concatenate([cum, steps[:, None]], axis=1)
    packed = packed.reshape(2, 3, length, chunks, per)
    aux = packed.transpose(0, 3, 2, 1, 4).reshape(2, chunks, length, 3 * per)
    rows = packed[:, :2].transpose(0, 3, 1, 4, 2).reshape(2, chunks, 2 * per, length)

    x, bc, bt, local = mix(value_in, bc_in, before, after, conv_value, conv_bc, aux, keep)
    entering = enter_states(local, log_total, width)
    y = scan_local(x, bc, bt, aux, rows, jnp.repeat(skip_gain, width)[None])
    normed = finish(y, bc, entering, aux, gate_in, out_gain[None])
    term = project_out(normed, w_out)
    return lax.psum_scatter(term, "head", scatter_dimension=1, tiled=True)


def solution(mesh):
    return jax.shard_map(
        shards,
        mesh=mesh,
        in_specs=(
            P("ctx", None),
            P("ctx"),
            P(),
            P(None, "head"),
            P(None, "head"),
            P(),
            P(None, "head"),
            P(None, "head"),
            P(),
            P("head"),
            P("head"),
            P("head"),
            P("head"),
            P("head", None),
        ),
        out_specs=P("ctx", "head"),
        check_vma=False,
    )
```

time: 1050 us -> 261 us (0.25); the launches traced: 1030 us -> 259 us
  waiting for transfers between devices: 560 us -> 73 us
  local copies, waits for them, and re-layouts: 220 us -> 9.35 us
  Pallas kernels: 0 us -> 102 us
  matrix products: 116 us -> 40.2 us
  other arithmetic: 77.2 us -> 6.55 us
  blocking collectives: 23.8 us -> 0 us
    ppermute x11 -> x8, waiting for transfers between devices: 380 us -> 18 us  [the longest x2 9.78 us: enter_states(): lax.ppermute((chip + chip_decay * entering.astype(F32)).astype(BF16), 'ct...]
    rev x9 -> x0, local copies, waits for them, and re-layouts: 147 us -> none  [the longest x1 67.7 us: shards(): term[1][::-1, ::-1]]
    pallas_call x0 -> x5, Pallas kernels: none -> 102 us  [the longest x1 31.6 us: scan_local(): pl.pallas_call(scan_kernel, grid=(2, chunks), in_specs=[pl.BlockSpec((1,...]
    dot_general x10 -> x5, matrix products: 116 us -> 40.2 us  [the longest x4 38.2 us: project(): jnp.einsum('btd,dk->btk', scaled, weight, preferred_element_type=F32)]
    reduce_scatter x2 -> x1, waiting for transfers between devices: 119 us -> 54.9 us  [shards(): return lax.psum_scatter(term, 'head', scatter_dimension=1, tiled=True)]
    all_gather x2 -> x0, waiting for transfers between devices: 59.7 us -> none  [prefix(): gathered = jax.tree.map(lambda a: lax.all_gather(a, axis), part)]
    add x10 -> x0, other arithmetic: 28.5 us -> none  [the longest x1 17.6 us: convolve(): forward_sum + kernel[offset] * padded[:, offset:offset + length]]
    all_gather x2 -> x0, blocking collectives: 23.8 us -> none  [prefix(): gathered = jax.tree.map(lambda a: lax.all_gather(a, axis), part)]
  transfers between devices with their start and end apart: 15 -> 9, of which waited for: 11 -> 5; matrix products, arithmetic and copies ran while one was open for 8% -> 11% of each run, Pallas kernels for 0% -> 12%
where the time goes in v1:
time: 261 us; the launch traced here: 259 us
  Pallas kernels  102 us (39%)
  waiting for transfers between devices  73 us (28%)
  matrix products  40.2 us (15%)
  starting transfers between devices  14.7 us (6%)
  between operations  13.8 us (5%)
  local copies, waits for them, and re-layouts  9.35 us (4%)
  other arithmetic  6.55 us (3%)
    reduce_scatter x1, waiting for transfers between devices, shards(): return lax.psum_scatter(term, 'head', scatter_dimension=1, tiled=True)  54.9 us
    dot_general x4, matrix products, project(): jnp.einsum('btd,dk->btk', scaled, weight, preferred_element_type=F32)  38.2 us
    pallas_call x1, Pallas kernels, scan_local(): pl.pallas_call(scan_kernel, grid=(2, chunks), in_specs=[pl.BlockSpec((1,...  31.6 us
    pallas_call x1, Pallas kernels, project_out(): pl.pallas_call(project_out_kernel, grid=(count,), in_specs=[pl.BlockSpec(...  23.2 us
    pallas_call x1, Pallas kernels, mix(): pl.pallas_call(mix_kernel, grid=(2, chunks + 1), in_specs=[pl.BlockSpec((...  20.6 us
    pallas_call x1, Pallas kernels, prepare(): pl.pallas_call(prepare_kernel, grid=(count,), in_specs=[pl.BlockSpec((len...  14 us
    pallas_call x1, Pallas kernels, finish(): pl.pallas_call(finish_kernel, grid=(2, chunks), in_specs=[pl.BlockSpec((1...  12.4 us
    ppermute x2, waiting for transfers between devices, enter_states(): lax.ppermute((chip + chip_decay * entering.astype(F32)).astype(BF16), 'ct...  9.78 us
  transfers between devices with their start and end apart: 9, of which 5 were waited for; matrix products, arithmetic and copies ran while one was open for 11% of the time, Pallas kernels for 12%

profile of v1, /device:TPU:0, one launch (start us, length us, event | category | flops | bytes accessed | tf_op | source)
XLA Modules:
  0.0 259.5 jit_solution(9083251289790692277)
XLA Ops:
  6.5 14.0 %prepare.1 = (bf16[2,512,4096]{2,1,0:T(8,128)(2,1)}, f32[512,128]{1,0:T(8,128)}) custom-call(bf16[512,4096]{1,0:T(8,128)(2,1)} %mirror_ref.2, bf16[512,4096]{1,0:T(8,128)(2,1)} %mirror_ref.2, f32[1,4096]{1,0:T(1,128)} %bitcast.64), custom_call_target="tpu_custom_call" | custom-call | tf_op jit(solution)/shard_map/prepare/pallas_call | solution.py:68
  20.5 1.1 reduce_sum.9
  21.7 5.9 %fusion.15.bc_ref = f32[2,512,256]{2,1,0:T(8,128)S(1)} fusion(bf16[2,512,4096]{2,1,0:T(8,128)(2,1)} %get-tuple-element.11, bf16[4096,256]{1,0:T(8,128)(2,1)S(1)} %copy-done, f32[512]{0:T(512)S(1)} %add_rsqrt_fusion), kind=kOutput, calls=%fused_computation.12 | convolution fusion | flops 2147745792 | bytes 11536384 | tf_op jit(solution)/shard_map/btd,dk->btk/dot_general | solution.py:394
  27.6 11.7 %fusion.4.v_ref = f32[2,512,1024]{2,1,0:T(8,128)S(1)} fusion(bf16[2,512,4096]{2,1,0:T(8,128)(2,1)S(1)} %copy-done.2, bf16[4096,1024]{1,0:T(8,128)(2,1)} %param.18, f32[512]{0:T(512)S(1)} %add_rsqrt_fusion), kind=kOutput, calls=%fused_computation.4 | convolution fusion | flops 8590983168 | bytes 20973568 | tf_op jit(solution)/shard_map/btd,dk->btk/dot_general | solution.py:394
  39.3 1.9 copy-done.3
  41.3 2.4 collective-permute-start
  43.7 1.5 collective-permute-start.1
  45.1 0.1 fusion.22
  45.3 0.9 copy.24.keep_ref
  46.2 5.7 %compare_select_fusion = f32[2,512,16]{1,2,0:T(8,128)S(1)} fusion(bf16[2,512,4096]{2,1,0:T(8,128)(2,1)} %get-tuple-element.11, bf16[4096,16]{0,1:T(8,128)(2,1)S(1)} %copy-done.5, f32[16]{0:T(128)S(1)} %copy-done.6, f32[512]{0:T(512)S(1)} %add_rsqrt_fusion), kind=kOutput, calls=%fused_computation.32 | convolution fusion | flops 134348800 | bytes 8587328 | tf_op jit(solution)/shard_map/btd,dk->btk/dot_general | solution.py:394
  52.0 2.0 fusion.18
  54.0 0.1 copy.21
  54.2 2.0 copy.23.aux_ref
  56.2 0.6 slice.48.before_bc
  56.8 0.6 slice.47.before_v
  57.4 0.6 slice.52.after_bc
  58.0 0.6 slice.51.after_v
  58.6 20.6 %mix.1 = (bf16[2,2,512,1024]{3,2,1,0:T(8,128)(2,1)}, bf16[2,2,512,256]{3,2,1,0:T(8,128)(2,1)}, bf16[2,2,128,512]{3,2,1,0:T(8,128)(2,1)}, f32[2,2,128,1024]{3,2,1,0:T(8,128)}) custom-call(f32[2,512,1024]{2,1,0:T(8,128)} %copy-done.3, f32[2,512,256]{2,1,0:T(8,128)} %copy-done.4, f32[2,8,1024]{2,1,0:T(8,128)} %slice.47.before_v, f32[2,8,256]{2,1,0:T(8,128)} %slice.48.before_bc, ...), custom_call_target="tpu_custom_call" | custom-call | flops 536870912 | bytes 14680064 | tf_op jit(solution)/shard_map/mix/pallas_call | solution.py:153
  79.2 1.7 fusion.24
  80.9 3.4 %collective-permute-start.3 = (bf16[2,128,1024]{2,1,0:T(8,128)(2,1)S(1)}, bf16[2,128,1024]{2,1,0:T(8,128)(2,1)S(1)}, u32[]{:S(2)}, u32[]{:S(2)}) collective-permute-start(bf16[2,128,1024]{2,1,0:T(8,128)(2,1)S(1)} %fusion.24), channel_id=1, source_target_pairs={{0,4},{4,0},{8,12},{12,8},{16,20},{20,16},{24,28},{28,24},{1,5},{5... | collective-permute-start | bytes 1572872 | tf_op jit(solution)/shard_map/ppermute | solution.py:366
  84.3 0.2 slice_reduce_fusion
  84.5 0.1 broadcast_in_dim.37
  84.6 0.1 mul.90
  84.6 1.2 collective-permute-done.3
  85.9 1.8 fusion.32
  87.7 1.3 collective-permute-start.4
  89.0 2.6 collective-permute-start.2
  91.5 0.8 collective-permute-done.2
  92.3 0.1 broadcast_in_dim.36
  92.4 0.1 mul.88
  92.5 6.2 %collective-permute-done.4 = bf16[2,128,1024]{2,1,0:T(8,128)(2,1)S(1)} collective-permute-done((bf16[2,128,1024]{2,1,0:T(8,128)(2,1)S(1)}, bf16[2,128,1024]{2,1,0:T(8,128)(2,1)S(1)}, u32[]{:S(2)}, u32[]{:S(2)}) %collective-permute-start.4) | collective-permute-done | bytes 524320 | tf_op jit(solution)/shard_map/ppermute | solution.py:368
  98.7 0.2 add_convert_fusion.1
  98.9 1.3 collective-permute-start.5
  100.2 9.8 %collective-permute-done.5 = bf16[2,128,1024]{2,1,0:T(8,128)(2,1)S(1)} collective-permute-done((bf16[2,128,1024]{2,1,0:T(8,128)(2,1)S(1)}, bf16[2,128,1024]{2,1,0:T(8,128)(2,1)S(1)}, u32[]{:S(2)}, u32[]{:S(2)}) %collective-permute-start.5) | collective-permute-done | bytes 524320 | tf_op jit(solution)/shard_map/ppermute | solution.py:370
  110.0 0.2 add_convert_fusion
  110.2 1.5 collective-permute-start.6
  111.7 15.0 %fusion.7.gate_ref = f32[2,512,1024]{2,1,0:T(8,128)} fusion(bf16[2,512,4096]{2,1,0:T(8,128)(2,1)} %get-tuple-element.11, bf16[4096,1024]{1,0:T(8,128)(2,1)} %param.17, f32[512]{0:T(512)S(1)} %add_rsqrt_fusion), kind=kOutput, calls=%fused_computation.5 | convolution fusion | flops 8590983168 | bytes 20973568 | tf_op jit(solution)/shard_map/btd,dk->btk/dot_general | solution.py:394
  126.7 0.1 broadcast_in_dim.35
  126.8 0.7 broadcast_in_dim_reshape.2.skip_ref
  127.4 0.7 reshape.65.row_ref
  128.1 0.8 collective-permute-start.7
  128.9 31.6 %scan_local.1.y_ref = f32[2,512,1024]{2,1,0:T(8,128)} custom-call(bf16[2,2,512,1024]{3,2,1,0:T(8,128)(2,1)} %get-tuple-element.13.x_ref, bf16[2,2,512,256]{3,2,1,0:T(8,128)(2,1)} %get-tuple-element.14.bc_ref, bf16[2,2,128,512]{3,2,1,0:T(8,128)(2,1)} %get-tuple-element.15.bt_ref, f32[2,4,512,12]{3,2,1,0:T(8,128)} %copy.23.aux_ref, ...), custom_call_target="tpu_custom_call" | custom-call | flops 8589934592 | bytes 10485760 | tf_op jit(solution)/shard_map/scan_local/pallas_call | solution.py:259
  160.6 0.3 select_bitcast_fusion.1
  160.9 1.1 pad_maximum_fusion.s_ref
  162.0 12.4 %finish.1.normed_ref = bf16[2,512,1024]{2,1,0:T(8,128)(2,1)} custom-call(f32[2,512,1024]{2,1,0:T(8,128)} %scan_local.1.y_ref, bf16[2,2,512,256]{3,2,1,0:T(8,128)(2,1)} %get-tuple-element.14.bc_ref, bf16[2,2,128,1024]{3,2,1,0:T(8,128)(2,1)} %pad_maximum_fusion.s_ref, f32[2,4,512,12]{3,2,1,0:T(8,128)} %copy.23.aux_ref, f32[2,512,1024]{2,1,0:T(8,128)} %fusion.7.gate_ref, ...), custom_call_target="tpu_custom_call" | custom-call | tf_op jit(solution)/shard_map/finish/pallas_call | solution.py:311
  174.4 23.2 %project_out.1 = bf16[512,4096]{1,0:T(8,128)(2,1)} custom-call(bf16[2,512,1024]{2,1,0:T(8,128)(2,1)} %finish.1.normed_ref, bf16[1024,4096]{1,0:T(8,128)(2,1)} %mirror_ref.3, bf16[1024,4096]{1,0:T(8,128)(2,1)} %mirror_ref.3), custom_call_target="tpu_custom_call" | custom-call | tf_op jit(solution)/shard_map/project_out/pallas_call | solution.py:340
  197.6 0.0 reduce-scatter.2.cloned.1.call-update
  197.7 54.9 %reduce-scatter.2.cloned.1.call-done = bf16[512,1024]{1,0:T(8,128)(2,1)} async-done(((bf16[512,4096]{1,0:T(8,128)(2,1)}), bf16[512,1024]{1,0:T(8,128)(2,1)}) %reduce-scatter.2.cloned.1.call-update) | async-done | bytes 1048592 | tf_op jit(solution)/shard_map/reduce_scatter | solution.py:425
  (39 shorter events, 0.3 us)
Async XLA Ops:
  6.5 15.1 %copy-start = (bf16[4096,256]{1,0:T(8,128)(2,1)S(1)}, bf16[4096,256]{1,0:T(8,128)(2,1)}, u32[]{:S(2)}) copy-start(bf16[4096,256]{1,0:T(8,128)(2,1)} %param.19) | copy-start | bytes 6291460
  6.5 246.1 %reduce-scatter.2.cloned.1.call-start = ((), (), s32[]{:S(2)}) async-start(), calls=%async_computation.1 | async-start | bytes 5242880 | tf_op jit(solution)/shard_map/reduce_scatter | solution.py:425
  21.7 5.9 %copy-start.2 = (bf16[2,512,4096]{2,1,0:T(8,128)(2,1)S(1)}, bf16[2,512,4096]{2,1,0:T(8,128)(2,1)}, u32[]{:S(2)}) copy-start(bf16[2,512,4096]{2,1,0:T(8,128)(2,1)} %get-tuple-element.11) | copy-start | bytes 25165828
  27.5 11.8 %copy-start.4 = (f32[2,512,256]{2,1,0:T(8,128)}, f32[2,512,256]{2,1,0:T(8,128)S(1)}, u32[]{:S(2)}) copy-start(f32[2,512,256]{2,1,0:T(8,128)S(1)} %fusion.15.bc_ref) | copy-start | bytes 3145732
  27.6 17.7 %copy-start.9 = (f32[16]{0:T(128)S(1)}, f32[16]{0:T(128)}, u32[]{:S(2)}) copy-start(f32[16]{0:T(128)} %param.24) | copy-start | bytes 196
  27.6 17.7 %copy-start.7 = (s32[512]{0:T(512)S(1)}, s32[512]{0:T(512)}, u32[]{:S(2)}) copy-start(s32[512]{0:T(512)} %param.15) | copy-start | bytes 6148
  27.6 18.6 %copy-start.5 = (bf16[4096,16]{0,1:T(8,128)(2,1)S(1)}, bf16[4096,16]{0,1:T(8,128)(2,1)}, u32[]{:S(2)}) copy-start(bf16[4096,16]{0,1:T(8,128)(2,1)} %param.20) | copy-start | bytes 393220
  27.6 18.6 %copy-start.6 = (f32[16]{0:T(128)S(1)}, f32[16]{0:T(128)}, u32[]{:S(2)}) copy-start(f32[16]{0:T(128)} %param.23) | copy-start | bytes 196
  39.3 1.9 copy-start.3
  41.3 14.9 %collective-permute-start = (f32[2,8,1280]{2,1,0:T(8,128)S(1)}, f32[2,8,1280]{2,1,0:T(8,128)S(1)}, u32[]{:S(2)}, u32[]{:S(2)}) collective-permute-start(f32[2,8,1280]{2,1,0:T(8,128)S(1)} %pad_maximum_fusion.2), channel_id=1, source_target_pairs={{0,4},{4,8},{8,12},{12,16},{16,20},{20,24},{24,28},{1,5},{5,9},{9,... | collective-permute-start | bytes 245768 | tf_op jit(solution)/shard_map/ppermute | solution.py:405
  43.7 13.7 %collective-permute-start.1 = (f32[2,8,1280]{2,1,0:T(8,128)S(1)}, f32[2,8,1280]{2,1,0:T(8,128)S(1)}, u32[]{:S(2)}, u32[]{:S(2)}) collective-permute-start(f32[2,8,1280]{2,1,0:T(8,128)S(1)} %pad_maximum_fusion.3), channel_id=1, source_target_pairs={{4,0},{8,4},{12,8},{16,12},{20,16},{24,20},{28,24},{5,1},{9,5},{13... | collective-permute-start | bytes 245768 | tf_op jit(solution)/shard_map/ppermute | solution.py:406
  80.9 4.9 %collective-permute-start.3 = (bf16[2,128,1024]{2,1,0:T(8,128)(2,1)S(1)}, bf16[2,128,1024]{2,1,0:T(8,128)(2,1)S(1)}, u32[]{:S(2)}, u32[]{:S(2)}) collective-permute-start(bf16[2,128,1024]{2,1,0:T(8,128)(2,1)S(1)} %fusion.24), channel_id=1, source_target_pairs={{0,4},{4,0},{8,12},{12,8},{16,20},{20,16},{24,28},{28,24},{1,5},{5... | collective-permute-start | bytes 1572872 | tf_op jit(solution)/shard_map/ppermute | solution.py:366
  87.7 11.1 %collective-permute-start.4 = (bf16[2,128,1024]{2,1,0:T(8,128)(2,1)S(1)}, bf16[2,128,1024]{2,1,0:T(8,128)(2,1)S(1)}, u32[]{:S(2)}, u32[]{:S(2)}) collective-permute-start(bf16[2,128,1024]{2,1,0:T(8,128)(2,1)S(1)} %get-tuple-element.17), channel_id=1, source_target_pairs={{4,12},{12,20},{20,28},{8,0},{16,8},{24,16},{5,13},{13,21},{21,29}... | collective-permute-start | bytes 1572872 | tf_op jit(solution)/shard_map/ppermute | solution.py:368
  89.0 3.4 %collective-permute-start.2 = (f32[2,16]{1,0:T(2,128)S(1)}, f32[2,16]{1,0:T(2,128)S(1)}, u32[]{:S(2)}, u32[]{:S(2)}) collective-permute-start(f32[2,16]{1,0:T(2,128)S(1)} %slice_reduce_fusion), channel_id=1, source_target_pairs={{0,4},{4,0},{8,12},{12,8},{16,20},{20,16},{24,28},{28,24},{1,5},{5... | collective-permute-start | bytes 392 | tf_op jit(solution)/shard_map/ppermute | solution.py:362
  98.9 11.1 %collective-permute-start.5 = (bf16[2,128,1024]{2,1,0:T(8,128)(2,1)S(1)}, bf16[2,128,1024]{2,1,0:T(8,128)(2,1)S(1)}, u32[]{:S(2)}, u32[]{:S(2)}) collective-permute-start(bf16[2,128,1024]{2,1,0:T(8,128)(2,1)S(1)} %add_convert_fusion.1), channel_id=1, source_target_pairs={{4,12},{12,20},{20,28},{8,0},{16,8},{24,16},{5,13},{13,21},{21,29}... | collective-permute-start | bytes 1572872 | tf_op jit(solution)/shard_map/ppermute | solution.py:370
  110.2 16.5 %copy-start.8 = (f32[16]{0:T(128)S(1)}, f32[16]{0:T(128)}, u32[]{:S(2)}) copy-start(f32[16]{0:T(128)} %param.25) | copy-start | bytes 196
  110.2 18.0 %collective-permute-start.6 = (bf16[2,128,1024]{2,1,0:T(8,128)(2,1)S(1)}, bf16[2,128,1024]{2,1,0:T(8,128)(2,1)S(1)}, u32[]{:S(2)}, u32[]{:S(2)}) collective-permute-start(bf16[2,128,1024]{2,1,0:T(8,128)(2,1)S(1)} %add_convert_fusion), channel_id=1, source_target_pairs={{4,12},{12,20},{20,28},{8,0},{16,8},{24,16},{5,13},{13,21},{21,29}... | collective-permute-start | bytes 1572872 | tf_op jit(solution)/shard_map/ppermute | solution.py:370
  128.1 32.4 %collective-permute-start.7 = (bf16[2,128,1024]{2,1,0:T(8,128)(2,1)S(1)}, bf16[2,128,1024]{2,1,0:T(8,128)(2,1)S(1)}, u32[]{:S(2)}, u32[]{:S(2)}) collective-permute-start(bf16[2,128,1024]{2,1,0:T(8,128)(2,1)S(1)} %collective-permute-done.6), channel_id=1, source_target_pairs={{0,4},{4,0},{8,12},{12,8},{16,20},{20,16},{24,28},{28,24},{1,5},{5... | collective-permute-start | bytes 1572872 | tf_op jit(solution)/shard_map/ppermute | solution.py:373
  174.4 78.2 %copy-start.1 = (bf16[4096,256]{1,0:T(8,128)(2,1)S(1)}, bf16[4096,256]{1,0:T(8,128)(2,1)}, u32[]{:S(2)}) copy-start(bf16[4096,256]{1,0:T(8,128)(2,1)} %param.19) | copy-start | bytes 6291460
Sparse Core Ops, SparseCore 0:
  197.8 54.7 reduce-scatter.1

commit v2 on v1

--- a/solution.py
+++ b/solution.py
@@ -188,7 +188,104 @@
     )(value_in, bc_in, before_v, before_bc, after_v, after_bc, conv_value, conv_bc, aux, keep)
 
 
-def scan_kernel(x_ref, bc_ref, bt_ref, aux_ref, row_ref, skip_ref, y_ref):
+def chain(size, last, local_ref, total_ref, ent_ref, swapped, decay_other, chip, kept,
+          hop_out, hop_in, crossed, send_sems, recv_sems):
+    me = lax.axis_index("ctx")
+    odd = lax.rem(me, 2)
+    hops = size // 2 - 1
+    ahead = me + 4 * odd - 2
+    behind = me - 4 * odd + 2
+    has_ahead = (ahead >= 0) & (ahead < size)
+    has_behind = (behind >= 0) & (behind < size)
+    partner = me + 1 - 2 * odd
+
+    def remote(source, target, index, device):
+        return pltpu.make_async_remote_copy(
+            src_ref=source,
+            dst_ref=target,
+            send_sem=send_sems.at[index],
+            recv_sem=recv_sems.at[index],
+            device_id={"ctx": device},
+            device_id_type=pl.DeviceIdType.MESH,
+        )
+
+    swap_copy = remote(kept, swapped, 0, partner)
+    decay_copy = remote(total_ref, decay_other, 1, partner)
+    cross_copy = remote(kept, crossed, 2, partner)
+    hop_copies = [remote(hop_out.at[k], hop_in.at[k], 3 + k, ahead) for k in range(hops)]
+
+    def greet():
+        barrier = pltpu.get_barrier_semaphore()
+
+        def signal(device):
+            pl.semaphore_signal(
+                barrier, inc=1, device_id={"ctx": device}, device_id_type=pl.DeviceIdType.MESH
+            )
+
+        signal(partner)
+        pl.when(has_ahead)(lambda: signal(ahead))
+        pl.when(has_behind)(lambda: signal(behind))
+        pl.semaphore_wait(
+            barrier, 1 + has_ahead.astype(jnp.int32) + has_behind.astype(jnp.int32)
+        )
+
+    def first():
+        greet()
+        for b in range(2):
+            kept[b] = jnp.where(odd == 1, local_ref[b, 1], local_ref[b, 0]).astype(BF16)
+        swap_copy.start()
+        decay_copy.start()
+
+    def second():
+        swap_copy.wait()
+        decay_copy.wait()
+        for b in range(2):
+            mine = jnp.where(odd == 1, local_ref[b, 0], local_ref[b, 1])
+            decay = jnp.exp(total_ref[b, :1])
+            chip[b] = decay * swapped[b].astype(F32) + mine
+            hop_out[0, b] = chip[b].astype(BF16)
+        pl.when(has_ahead)(lambda: hop_copies[0].start())
+
+    def entered(k, b):
+        return jnp.where(has_behind, hop_in[k, b].astype(F32), 0.0)
+
+    def hop(k):
+        def stage():
+            pl.when(has_behind)(lambda: hop_copies[k - 1].wait_recv())
+            for b in range(2):
+                decay = jnp.exp(total_ref[b, :1] + decay_other[b, :1])
+                hop_out[k, b] = (chip[b] + decay * entered(k - 1, b)).astype(BF16)
+            pl.when(has_ahead)(lambda: hop_copies[k].start())
+
+        return stage
+
+    def cross():
+        pl.when(has_behind)(lambda: hop_copies[hops - 1].wait_recv())
+        for b in range(2):
+            kept[b] = entered(hops - 1, b).astype(BF16)
+        cross_copy.start()
+
+    def end():
+        cross_copy.wait()
+        for b in range(2):
+            own = jnp.exp(decay_other[b, :1]) * kept[b].astype(F32) + swapped[b].astype(F32)
+            other = crossed[b].astype(F32)
+            ent_ref[b, 0] = jnp.where(odd == 1, own, other).astype(BF16)
+            ent_ref[b, 1] = jnp.where(odd == 1, other, own).astype(BF16)
+        for k in range(hops):
+            pl.when(has_ahead)(lambda k=k: hop_copies[k].wait_send())
+
+    stages = [first, second] + [hop(k) for k in range(1, hops)] + [cross]
+    return [(min(last, (7 * i) // 5), stage) for i, stage in enumerate(stages)], end
+
+
+def scan_kernel(size, x_ref, bc_ref, bt_ref, aux_ref, row_ref, skip_ref, local_ref, total_ref,
+                y_ref, ent_ref, *scratch):
+    step = pl.program_id(0) * pl.num_programs(1) + pl.program_id(1)
+    last_step = 2 * (local_ref.shape[3] // COLS) - 1
+    stages, end = chain(size, last_step, local_ref, total_ref, ent_ref, *scratch)
+    for at, stage in stages:
+        pl.when(step == at)(stage)
     length = x_ref.shape[2]
     state = bt_ref.shape[2]
     heads = aux_ref.shape[3] // 3
@@ -249,15 +346,19 @@
                     carried = decay[:1] * carried + fresh
                 else:
                     carried = fresh
-
-
-def scan_local(x, bc, bt, aux, rows, skip):
+    pl.when(step == last_step)(end)
+
+
+def scan_local(x, bc, bt, aux, rows, skip, local, total):
+    size = lax.axis_size("ctx")
+    hops = size // 2 - 1
+    wide = local.shape[2:]
     _, _, length, inner = x.shape
     pair = bc.shape[3]
     state = pair // 2
     chunks = inner // COLS
     return pl.pallas_call(
-        scan_kernel,
+        functools.partial(scan_kernel, size),
         grid=(2, chunks),
         in_specs=[
             pl.BlockSpec((1, 2, length, COLS), lambda b, c: (b, 0, 0, c)),
@@ -266,17 +367,41 @@
             pl.BlockSpec((1, 1) + aux.shape[2:], lambda b, c: (b, c, 0, 0)),
             pl.BlockSpec((1, 1) + rows.shape[2:], lambda b, c: (b, c, 0, 0)),
             pl.BlockSpec((1, COLS), lambda b, c: (0, c)),
-        ],
-        out_specs=pl.BlockSpec((1, length, COLS), lambda b, c: (b, 0, c)),
-        out_shape=jax.ShapeDtypeStruct((2, length, inner), F32),
-        compiler_params=params(2),
+            pl.BlockSpec(local.shape, lambda b, c: (0, 0, 0, 0)),
+            pl.BlockSpec(total.shape, lambda b, c: (0, 0, 0)),
+        ],
+        out_specs=[
+            pl.BlockSpec((1, length, COLS), lambda b, c: (b, 0, c)),
+            pl.BlockSpec(local.shape, lambda b, c: (0, 0, 0, 0)),
+        ],
+        out_shape=[
+            jax.ShapeDtypeStruct((2, length, inner), F32),
+            jax.ShapeDtypeStruct(local.shape, BF16),
+        ],
+        scratch_shapes=[
+            pltpu.VMEM((2,) + wide, BF16),
+            pltpu.VMEM(total.shape, F32),
+            pltpu.VMEM((2,) + wide, F32),
+            pltpu.VMEM((2,) + wide, BF16),
+            pltpu.VMEM((hops, 2) + wide, BF16),
+            pltpu.VMEM((hops, 2) + wide, BF16),
+            pltpu.VMEM((2,) + wide, BF16),
+            pltpu.SemaphoreType.DMA((3 + hops,)),
+            pltpu.SemaphoreType.DMA((3 + hops,)),
+        ],
+        compiler_params=pltpu.CompilerParams(
+            vmem_limit_bytes=VMEM_LIMIT,
+            dimension_semantics=("arbitrary",) * 2,
+            collective_id=1,
+            has_side_effects=True,
+        ),
         cost_estimate=pl.CostEstimate(
             flops=2 * 64 * length * ROWS * inner,
             bytes_accessed=20 * length * inner,
             transcendentals=0,
         ),
         name="scan_local",
-    )(x, bc, bt, aux, rows, skip)
+    )(x, bc, bt, aux, rows, skip, local, total)
 
 
 def finish_kernel(y_ref, bc_ref, s_ref, aux_ref, gate_ref, gain_ref, out_ref):
@@ -326,53 +451,117 @@
     )(y, bc, entering, aux, gate_in, gain)
 
 
-def project_out_kernel(normed_ref, own_ref, mirror_ref, out_ref):
-    flipped = matmul(mirror_ref[...], anti_identity(COLS)).astype(BF16)
-    out_ref[...] = (
-        matmul(normed_ref[0], own_ref[...]) + matmul(normed_ref[1], flipped)
-    ).astype(BF16)
+def project_out_kernel(
+    count, normed_ref, w_ref, out_ref, held, sending, landed, send_sems, recv_sems
+):
+    me = lax.axis_index("head")
+    bits = count.bit_length() - 1
+    inner, depth = w_ref.shape
+    half = depth // count // 2
+    tile = min(half, COLS)
+    orders = (list(range(bits)), list(range(bits))[::-1])
+
+    barrier = pltpu.get_barrier_semaphore()
+    for bit in range(bits):
+        pl.semaphore_signal(
+            barrier, inc=1, device_id={"head": me ^ (1 << bit)},
+            device_id_type=pl.DeviceIdType.MESH,
+        )
+    pl.semaphore_wait(barrier, bits)
+
+    def phase_of(side, mask):
+        return next(p for p, bit in enumerate(orders[side]) if mask >> bit & 1)
+
+    def copy_of(side, mask):
+        slot = side * (count - 1) + mask - 1
+        partner = me ^ (1 << orders[side][phase_of(side, mask)])
+        return pltpu.make_async_remote_copy(
+            src_ref=sending.at[slot],
+            dst_ref=landed.at[slot],
+            send_sem=send_sems.at[slot],
+            recv_sem=recv_sems.at[slot],
+            device_id={"head": partner},
+            device_id_type=pl.DeviceIdType.MESH,
+        )
+
+    def partial(side, mask, store):
+        first = (me ^ mask) * (2 * half) + side * half
+        flip = anti_identity(tile)
+
+        def one(j, carry):
+            at = pl.multiple_of(first + j * tile, tile)
+            mirrored = pl.multiple_of(depth - tile - at, tile)
+            flipped = matmul(w_ref[:, pl.ds(mirrored, tile)], flip).astype(BF16)
+            value = matmul(normed_ref[0], w_ref[:, pl.ds(at, tile)]) + matmul(
+                normed_ref[1], flipped
+            )
+            store(pl.ds(pl.multiple_of(j * tile, tile), tile), value)
+            return carry
+
+        lax.fori_loop(0, half // tile, one, 0)
+
+    def into_sending(slot):
+        def store(columns, value):
+            sending[slot, :, columns] = value.astype(BF16)
+
+        return store
+
+    def into_held(slot):
+        def store(columns, value):
+            held[slot, :, columns] = value
+
+        return store
+
+    pieces = sorted(
+        ((phase_of(side, mask), -bin(mask).count("1"), mask, side)
+         for side in range(2) for mask in range(1, count)),
+        key=lambda piece: piece[:2],
+    )
+    later = [(side, mask) for phase, _, mask, side in pieces if phase > 0] + [(0, 0), (1, 0)]
+    for phase, _, mask, side in pieces:
+        if phase == 0:
+            partial(side, mask, into_sending(side * (count - 1) + mask - 1))
+            copy_of(side, mask).start()
+    for place, (side, mask) in enumerate(later):
+        partial(side, mask, into_held(place))
+    for place, (side, mask) in enumerate(later):
+        total = held[place]
+        for q in range(phase_of(side, mask) if mask else bits):
+            source = mask | 1 << orders[side][q]
+            copy_of(side, source).wait_recv()
+            total = total + landed[side * (count - 1) + source - 1].astype(F32)
+        if mask:
+            sending[side * (count - 1) + mask - 1] = total.astype(BF16)
+            copy_of(side, mask).start()
+        else:
+            out_ref[:, side * half : (side + 1) * half] = total.astype(BF16)
+    for _, _, mask, side in pieces:
+        copy_of(side, mask).wait_send()
 
 
 def project_out(normed, w_out):
     _, length, inner = normed.shape
     depth = w_out.shape[1]
-    count = depth // COLS
+    count = lax.axis_size("head")
+    half = depth // count // 2
+    slots = 2 * (count - 1)
     return pl.pallas_call(
-        project_out_kernel,
-        grid=(count,),
-        in_specs=[
-            pl.BlockSpec((2, length, inner), lambda j: (0, 0, 0)),
-            pl.BlockSpec((inner, COLS), lambda j: (0, j)),
-            pl.BlockSpec((inner, COLS), lambda j: (0, count - 1 - j)),
-        ],
-        out_specs=pl.BlockSpec((length, COLS), lambda j: (0, j)),
-        out_shape=jax.ShapeDtypeStruct((length, depth), BF16),
-        compiler_params=params(1),
+        functools.partial(project_out_kernel, count),
+        in_specs=[pl.BlockSpec(memory_space=pltpu.VMEM)] * 2,
+        out_specs=pl.BlockSpec(memory_space=pltpu.VMEM),
+        out_shape=jax.ShapeDtypeStruct((length, depth // count), BF16),
+        scratch_shapes=[
+            pltpu.VMEM((count, length, half), F32),
+            pltpu.VMEM((slots, length, half), BF16),
+            pltpu.VMEM((slots, length, half), BF16),
+            pltpu.SemaphoreType.DMA((slots,)),
+            pltpu.SemaphoreType.DMA((slots,)),
+        ],
+        compiler_params=pltpu.CompilerParams(
+            vmem_limit_bytes=40 * 1024 * 1024, collective_id=0, has_side_effects=True
+        ),
         name="project_out",
-    )(normed, w_out, w_out)
-
-
-def enter_states(local, log_total, width):
-    size = lax.axis_size("ctx")
-    odd = lax.axis_index("ctx") % 2 == 1
-    swap = [(i, i ^ 1) for i in range(size)]
-    ahead = [(i, i + 2) for i in range(1, size - 2, 2)] + [(i, i - 2) for i in range(2, size, 2)]
-    decay = jnp.repeat(jnp.exp(log_total), width, axis=-1)[:, None, :]
-    other_decay = jnp.repeat(
-        jnp.exp(lax.ppermute(log_total, "ctx", swap)), width, axis=-1
-    )[:, None, :]
-    chip_decay = decay * other_decay
-    forward, backward = local[:, 0], local[:, 1]
-    received = lax.ppermute(jnp.where(odd, backward, forward).astype(BF16), "ctx", swap).astype(F32)
-    chip = decay * received + jnp.where(odd, forward, backward)
-    entering = lax.ppermute(chip.astype(BF16), "ctx", ahead)
-    for _ in range(size // 2 - 2):
-        entering = lax.ppermute(
-            (chip + chip_decay * entering.astype(F32)).astype(BF16), "ctx", ahead
-        )
-    crossed = lax.ppermute(entering, "ctx", swap)
-    own = (other_decay * entering.astype(F32) + received).astype(BF16)
-    return jnp.stack([jnp.where(odd, own, crossed), jnp.where(odd, crossed, own)], axis=1)
+    )(normed, w_out)
 
 
 def shards(
@@ -418,11 +607,12 @@
     rows = packed[:, :2].transpose(0, 3, 1, 4, 2).reshape(2, chunks, 2 * per, length)
 
     x, bc, bt, local = mix(value_in, bc_in, before, after, conv_value, conv_bc, aux, keep)
-    entering = enter_states(local, log_total, width)
-    y = scan_local(x, bc, bt, aux, rows, jnp.repeat(skip_gain, width)[None])
+    total = jnp.broadcast_to(jnp.repeat(log_total, width, axis=-1)[:, None], (2, 8, inner))
+    y, entering = scan_local(
+        x, bc, bt, aux, rows, jnp.repeat(skip_gain, width)[None], local, total
+    )
     normed = finish(y, bc, entering, aux, gate_in, out_gain[None])
-    term = project_out(normed, w_out)
-    return lax.psum_scatter(term, "head", scatter_dimension=1, tiled=True)
+    return project_out(normed, w_out)
 
 
 def solution(mesh):

time: 261 us -> 192 us (0.74)
  waiting for transfers between devices: 73 us -> 0.01 us
  Pallas kernels: 102 us -> 131 us
  between operations: 13.8 us -> 0.31 us
  starting transfers between devices: 14.7 us -> 3.65 us
  local copies, waits for them, and re-layouts: 9.35 us -> 15.8 us
  other arithmetic: 6.55 us -> 1.31 us
  matrix products: 40.2 us -> 36.9 us
    reduce_scatter x1 -> x0, waiting for transfers between devices: 54.9 us -> none  [shards(): return lax.psum_scatter(term, 'head', scatter_dimension=1, tiled=True)]
    pallas_call x2, Pallas kernels: 54.9 us -> 83.4 us  [the longest x1 49.7 us: scan_local(): pl.pallas_call(functools.partial(scan_kernel, size), grid=(2, chunks), in...]
    ppermute x6 -> x0, waiting for transfers between devices: 18 us -> none  [the longest x2 9.78 us: enter_states(): lax.ppermute((chip + chip_decay * entering.astype(F32)).astype(BF16), 'ct...]
    ppermute x6 -> x0, starting transfers between devices: 10.8 us -> none  [the longest x1 3.37 us: enter_states(): lax.ppermute(jnp.where(odd, backward, forward).astype(BF16), 'ctx', swap)]
    unnamed x20 -> x25, local copies, waits for them, and re-layouts: 1.96 us -> 7.92 us
    convert_element_type x4 -> x0, other arithmetic: 3.83 us -> none  [the longest x1 1.8 us: enter_states(): entering = lax.ppermute(chip.astype(BF16), 'ctx', ahead)]
    dot_general x4, matrix products: 38.2 us -> 34.8 us  [project(): jnp.einsum('btd,dk->btk', scaled, weight, preferred_element_type=F32)]
  transfers between devices with their start and end apart: 9 -> 2, of which waited for: 5 -> 0; matrix products, arithmetic and copies ran while one was open for 11% -> 14% of each run, Pallas kernels for 12% -> 0%
where the time goes in v2:
time: 192 us; the launch traced here: 189 us
  Pallas kernels  131 us (68%)
  matrix products  36.9 us (19%)
  local copies, waits for them, and re-layouts  15.8 us (8%)
  starting transfers between devices  3.65 us (2%)
    pallas_call x1, Pallas kernels, scan_local(): pl.pallas_call(functools.partial(scan_kernel, size), grid=(2, chunks), in...  49.7 us
    dot_general x4, matrix products, project(): jnp.einsum('btd,dk->btk', scaled, weight, preferred_element_type=F32)  34.8 us
    pallas_call x1, Pallas kernels, project_out(): pl.pallas_call(functools.partial(project_out_kernel, count), in_specs=[pl...  33.7 us
    pallas_call x1, Pallas kernels, mix(): pl.pallas_call(mix_kernel, grid=(2, chunks + 1), in_specs=[pl.BlockSpec((...  20.6 us
    pallas_call x1, Pallas kernels, prepare(): pl.pallas_call(prepare_kernel, grid=(count,), in_specs=[pl.BlockSpec((len...  14 us
    pallas_call x1, Pallas kernels, finish(): pl.pallas_call(finish_kernel, grid=(2, chunks), in_specs=[pl.BlockSpec((1...  12.6 us
    unnamed x25, local copies, waits for them, and re-layouts  7.92 us
  transfers between devices with their start and end apart: 2, of which 0 were waited for; matrix products, arithmetic and copies ran while one was open for 14% of the time, Pallas kernels for 0%

profile of v2, /device:TPU:0, one launch (start us, length us, event | category | flops | bytes accessed | tf_op | source)
XLA Modules:
  0.0 188.5 jit_solution(13163553626035931253)
XLA Ops:
  0.0 0.0 copy-start
  0.0 14.0 %prepare.1 = (bf16[2,512,4096]{2,1,0:T(8,128)(2,1)}, f32[512,128]{1,0:T(8,128)}) custom-call(bf16[512,4096]{1,0:T(8,128)(2,1)} %mirror_ref.1, bf16[512,4096]{1,0:T(8,128)(2,1)} %mirror_ref.1, f32[1,4096]{1,0:T(1,128)} %bitcast.53), custom_call_target="tpu_custom_call" | custom-call | tf_op jit(solution)/shard_map/prepare/pallas_call | solution.py:68
  14.0 1.1 reduce_sum.9
  15.1 0.0 copy-done
  15.2 0.0 copy-start.4
  15.2 5.9 %fusion.15.bc_ref = f32[2,512,256]{2,1,0:T(8,128)S(1)} fusion(bf16[2,512,4096]{2,1,0:T(8,128)(2,1)} %get-tuple-element.13, bf16[4096,256]{1,0:T(8,128)(2,1)S(1)} %copy-done, f32[512]{0:T(512)S(1)} %add_rsqrt_fusion), kind=kOutput, calls=%fused_computation.12 | convolution fusion | flops 2147745792 | bytes 11536384 | tf_op jit(solution)/shard_map/btd,dk->btk/dot_general | solution.py:583
  21.0 0.0 copy-start.6
  21.1 0.0 copy-done.4
  21.1 0.0 copy-start.11
  21.1 0.0 copy-start.7
  21.1 0.0 copy-start.8
  21.1 11.6 %fusion.4.v_ref = f32[2,512,1024]{2,1,0:T(8,128)S(1)} fusion(bf16[2,512,4096]{2,1,0:T(8,128)(2,1)S(1)} %copy-done.4, bf16[4096,1024]{1,0:T(8,128)(2,1)} %param.18, f32[512]{0:T(512)S(1)} %add_rsqrt_fusion), kind=kOutput, calls=%fused_computation.4 | convolution fusion | flops 8590983168 | bytes 20973568 | tf_op jit(solution)/shard_map/btd,dk->btk/dot_general | solution.py:583
  32.7 0.0 copy-done.6
  32.7 0.0 copy-start.5
  32.7 1.9 %copy-done.5 = f32[2,512,1024]{2,1,0:T(8,128)} copy-done((f32[2,512,1024]{2,1,0:T(8,128)}, f32[2,512,1024]{2,1,0:T(8,128)S(1)}, u32[]{:S(2)}) %copy-start.5) | copy-done | bytes 4194328
  34.7 2.4 %collective-permute-start = (f32[2,8,1280]{2,1,0:T(8,128)S(1)}, f32[2,8,1280]{2,1,0:T(8,128)S(1)}, u32[]{:S(2)}, u32[]{:S(2)}) collective-permute-start(f32[2,8,1280]{2,1,0:T(8,128)S(1)} %pad_maximum_fusion.1), channel_id=1, source_target_pairs={{0,4},{4,8},{8,12},{12,16},{16,20},{20,24},{24,28},{1,5},{5,9},{9,... | collective-permute-start | bytes 245768 | tf_op jit(solution)/shard_map/ppermute | solution.py:594
  37.1 1.3 collective-permute-start.1
  38.4 0.1 fusion.20
  38.5 0.0 copy-done.11
  38.6 0.0 copy-start.9
  38.6 0.0 copy-start.10
  38.6 2.3 %compare_select_fusion = f32[2,512,16]{1,2,0:T(8,128)S(1)} fusion(bf16[2,512,4096]{2,1,0:T(8,128)(2,1)S(1)} %copy-done.4, bf16[4096,16]{0,1:T(8,128)(2,1)S(1)} %copy-done.7, f32[16]{0:T(128)S(1)} %copy-done.8, f32[512]{0:T(512)S(1)} %add_rsqrt_fusion), kind=kOutput, calls=%fused_computation.21 | convolution fusion | flops 134348800 | bytes 8587328 | tf_op jit(solution)/shard_map/btd,dk->btk/dot_general | solution.py:583
  40.9 2.1 %fusion.18 = f32[2,2,512,16]{2,3,1,0:T(8,128)S(1)} fusion(f32[1,512,512]{2,1,0:T(8,128)S(1)} %get-tuple-element.26, f32[1,512,512]{2,1,0:T(8,128)S(1)} %get-tuple-element.25, f32[2,512,16]{1,2,0:T(8,128)S(1)} %compare_select_fusion, f32[16]{0:T(128)S(1)} %neg.7), kind=kOutput, calls=%fused_computation.13 | convolution fusion | flops 201867264 | bytes 2293824 | tf_op jit(solution)/shard_map/dts,bsh->bdth/dot_general | solution.py:602
  43.0 0.2 slice_reduce_fusion
  43.2 0.1 copy.18
  43.3 0.1 broadcast_in_dim.39
  43.4 0.7 broadcast_in_dim_reshape.4.skip_ref
  44.0 0.9 copy.21.keep_ref
  44.9 0.1 broadcast_in_dim.40
  45.0 0.1 broadcast_in_dim.41
  45.1 0.7 reshape.47.row_ref
  45.8 15.0 %fusion.7.gate_ref = f32[2,512,1024]{2,1,0:T(8,128)} fusion(bf16[2,512,4096]{2,1,0:T(8,128)(2,1)} %get-tuple-element.13, bf16[4096,1024]{1,0:T(8,128)(2,1)} %param.17, f32[512]{0:T(512)S(1)} %add_rsqrt_fusion), kind=kOutput, calls=%fused_computation.5 | convolution fusion | flops 8590983168 | bytes 20973568 | tf_op jit(solution)/shard_map/btd,dk->btk/dot_general | solution.py:583
  60.9 2.0 %copy.20.aux_ref = f32[2,4,512,12]{3,2,1,0:T(8,128)} copy(f32[2,4,512,12]{2,1,3,0:T(4,128)S(1)} %bitcast.51) | data formatting | bytes 393216 | tf_op jit(solution)/shard_map/reshape | solution.py:606
  62.9 0.0 collective-permute-done
  62.9 0.6 slice.40.before_bc
  63.5 0.6 slice.39.before_v
  64.1 0.0 collective-permute-done.1
  64.1 0.6 slice.44.after_bc
  64.7 0.6 slice.43.after_v
  65.3 20.6 %mix.1 = (bf16[2,2,512,1024]{3,2,1,0:T(8,128)(2,1)}, bf16[2,2,512,256]{3,2,1,0:T(8,128)(2,1)}, bf16[2,2,128,512]{3,2,1,0:T(8,128)(2,1)}, f32[2,2,128,1024]{3,2,1,0:T(8,128)}) custom-call(f32[2,512,1024]{2,1,0:T(8,128)} %copy-done.5, f32[2,512,256]{2,1,0:T(8,128)} %copy-done.6, f32[2,8,1024]{2,1,0:T(8,128)} %slice.39.before_v, f32[2,8,256]{2,1,0:T(8,128)} %slice.40.before_bc, ...), custom_call_target="tpu_custom_call" | custom-call | flops 536870912 | bytes 14680064 | tf_op jit(solution)/shard_map/mix/pallas_call | solution.py:153
  86.0 0.6 broadcast_in_dim.42.total_ref
  86.6 49.7 %scan_local.1 = (f32[2,512,1024]{2,1,0:T(8,128)}, bf16[2,2,128,1024]{3,2,1,0:T(8,128)(2,1)}) custom-call(bf16[2,2,512,1024]{3,2,1,0:T(8,128)(2,1)} %get-tuple-element.15.x_ref, bf16[2,2,512,256]{3,2,1,0:T(8,128)(2,1)} %get-tuple-element.16.bc_ref, bf16[2,2,128,512]{3,2,1,0:T(8,128)(2,1)} %get-tuple-element.17.bt_ref, f32[2,4,512,12]{3,2,1,0:T(8,128)} %copy.20.aux_ref, ...), custom_call_target="tpu_custom_call" | custom-call | flops 8589934592 | bytes 10485760 | tf_op jit(solution)/shard_map/scan_local/pallas_call | solution.py:360
  136.3 0.0 copy-start.1
  136.3 12.6 %finish.1.normed_ref = bf16[2,512,1024]{2,1,0:T(8,128)(2,1)} custom-call(f32[2,512,1024]{2,1,0:T(8,128)} %get-tuple-element.19.y_ref, bf16[2,2,512,256]{3,2,1,0:T(8,128)(2,1)} %get-tuple-element.16.bc_ref, bf16[2,2,128,1024]{3,2,1,0:T(8,128)(2,1)} %get-tuple-element.20.s_ref, f32[2,4,512,12]{3,2,1,0:T(8,128)} %copy.20.aux_ref, ...), custom_call_target="tpu_custom_call" | custom-call | tf_op jit(solution)/shard_map/finish/pallas_call | solution.py:436
  148.9 3.4 %copy-done.2 = bf16[1024,4096]{1,0:T(8,128)(2,1)S(1)} copy-done((bf16[1024,4096]{1,0:T(8,128)(2,1)S(1)}, bf16[1024,4096]{1,0:T(8,128)(2,1)}, u32[]{:S(2)}) %copy-start.2) | copy-done | bytes 8388632
  152.3 1.6 copy-done.3
  153.9 33.7 %project_out.1 = bf16[512,1024]{1,0:T(8,128)(2,1)S(1)} custom-call(bf16[2,512,1024]{2,1,0:T(8,128)(2,1)S(1)} %copy-done.3, bf16[1024,4096]{1,0:T(8,128)(2,1)S(1)} %copy-done.2), custom_call_target="tpu_custom_call" | custom-call | tf_op jit(solution)/shard_map/project_out/pallas_call | solution.py:548
  187.6 1.0 copy.29
  (19 shorter events, 0.2 us)
Async XLA Ops:
  0.0 15.1 %copy-start = (bf16[4096,256]{1,0:T(8,128)(2,1)S(1)}, bf16[4096,256]{1,0:T(8,128)(2,1)}, u32[]{:S(2)}) copy-start(bf16[4096,256]{1,0:T(8,128)(2,1)} %param.19) | copy-start | bytes 6291460
  15.2 5.9 %copy-start.4 = (bf16[2,512,4096]{2,1,0:T(8,128)(2,1)S(1)}, bf16[2,512,4096]{2,1,0:T(8,128)(2,1)}, u32[]{:S(2)}) copy-start(bf16[2,512,4096]{2,1,0:T(8,128)(2,1)} %get-tuple-element.13) | copy-start | bytes 25165828
  21.0 11.7 %copy-start.6 = (f32[2,512,256]{2,1,0:T(8,128)}, f32[2,512,256]{2,1,0:T(8,128)S(1)}, u32[]{:S(2)}) copy-start(f32[2,512,256]{2,1,0:T(8,128)S(1)} %fusion.15.bc_ref) | copy-start | bytes 3145732
  21.1 17.4 %copy-start.11 = (f32[16]{0:T(128)S(1)}, f32[16]{0:T(128)}, u32[]{:S(2)}) copy-start(f32[16]{0:T(128)} %param.24) | copy-start | bytes 196
  21.1 17.4 %copy-start.7 = (bf16[4096,16]{0,1:T(8,128)(2,1)S(1)}, bf16[4096,16]{0,1:T(8,128)(2,1)}, u32[]{:S(2)}) copy-start(bf16[4096,16]{0,1:T(8,128)(2,1)} %param.20) | copy-start | bytes 393220
  21.1 17.4 %copy-start.8 = (f32[16]{0:T(128)S(1)}, f32[16]{0:T(128)}, u32[]{:S(2)}) copy-start(f32[16]{0:T(128)} %param.23) | copy-start | bytes 196
  32.7 1.9 %copy-start.5 = (f32[2,512,1024]{2,1,0:T(8,128)}, f32[2,512,1024]{2,1,0:T(8,128)S(1)}, u32[]{:S(2)}) copy-start(f32[2,512,1024]{2,1,0:T(8,128)S(1)} %fusion.4.v_ref) | copy-start | bytes 12582916
  34.7 28.2 %collective-permute-start = (f32[2,8,1280]{2,1,0:T(8,128)S(1)}, f32[2,8,1280]{2,1,0:T(8,128)S(1)}, u32[]{:S(2)}, u32[]{:S(2)}) collective-permute-start(f32[2,8,1280]{2,1,0:T(8,128)S(1)} %pad_maximum_fusion.1), channel_id=1, source_target_pairs={{0,4},{4,8},{8,12},{12,16},{16,20},{20,24},{24,28},{1,5},{5,9},{9,... | collective-permute-start | bytes 245768 | tf_op jit(solution)/shard_map/ppermute | solution.py:594
  37.1 27.0 %collective-permute-start.1 = (f32[2,8,1280]{2,1,0:T(8,128)S(1)}, f32[2,8,1280]{2,1,0:T(8,128)S(1)}, u32[]{:S(2)}, u32[]{:S(2)}) collective-permute-start(f32[2,8,1280]{2,1,0:T(8,128)S(1)} %pad_maximum_fusion.2), channel_id=1, source_target_pairs={{4,0},{8,4},{12,8},{16,12},{20,16},{24,20},{28,24},{5,1},{9,5},{13... | collective-permute-start | bytes 245768 | tf_op jit(solution)/shard_map/ppermute | solution.py:595
  38.6 4.7 %copy-start.9 = (s32[512]{0:T(512)S(1)}, s32[512]{0:T(512)}, u32[]{:S(2)}) copy-start(s32[512]{0:T(512)} %param.15) | copy-start | bytes 6148
  38.6 4.7 %copy-start.10 = (f32[16]{0:T(128)S(1)}, f32[16]{0:T(128)}, u32[]{:S(2)}) copy-start(f32[16]{0:T(128)} %param.25) | copy-start | bytes 196
  136.3 52.3 %copy-start.1 = (bf16[4096,256]{1,0:T(8,128)(2,1)S(1)}, bf16[4096,256]{1,0:T(8,128)(2,1)}, u32[]{:S(2)}) copy-start(bf16[4096,256]{1,0:T(8,128)(2,1)} %param.19) | copy-start | bytes 6291460
  148.9 3.4 %copy-start.2 = (bf16[1024,4096]{1,0:T(8,128)(2,1)S(1)}, bf16[1024,4096]{1,0:T(8,128)(2,1)}, u32[]{:S(2)}) copy-start(bf16[1024,4096]{1,0:T(8,128)(2,1)} %w_ref.1) | copy-start | bytes 25165828
  152.3 1.6 copy-start.3

commit v3 on v2

--- a/solution.py
+++ b/solution.py
@@ -37,44 +37,56 @@
     heads = per_head.shape[1]
     high = per_head.astype(BF16)
     low = (per_head - high.astype(F32)).astype(BF16)
-    row = lax.broadcasted_iota(jnp.int32, (heads, heads * width), 0)
-    col = lax.broadcasted_iota(jnp.int32, (heads, heads * width), 1)
+    row = lax.broadcasted_iota(jnp.int32, (2 * heads, heads * width), 0)
+    col = lax.broadcasted_iota(jnp.int32, (2 * heads, heads * width), 1)
+    row = jnp.where(row < heads, row, row - heads)
     pick = ((col >= row * width) & (col < (row + 1) * width)).astype(F32).astype(BF16)
-    return matmul(high, pick) + matmul(low, pick)
+    return matmul(jnp.concatenate([high, low], axis=1), pick)
 
 
 def silu(x):
-    return x * (1.0 / (1.0 + jnp.exp(-x)))
+    half = 0.5 * x
+    return half + half * jnp.tanh(half)
 
 
 def prepare_kernel(own_ref, mirror_ref, gain_ref, scaled_ref, squares_ref):
-    own = own_ref[...].astype(F32)
-    gain = gain_ref[...]
-    scaled_ref[0] = (own * gain).astype(BF16)
-    flipped = matmul(mirror_ref[...], anti_identity(COLS))
-    scaled_ref[1] = (flipped * gain).astype(BF16)
+    flip = anti_identity(COLS)
+    parts = own_ref.shape[1] // COLS
+    squares = None
+    for q in range(parts):
+        at = slice(q * COLS, (q + 1) * COLS)
+        opposite = slice((parts - 1 - q) * COLS, (parts - q) * COLS)
+        own = own_ref[:, at].astype(F32)
+        gain = gain_ref[:, at]
+        scaled_ref[0, :, at] = (own * gain).astype(BF16)
+        scaled_ref[1, :, at] = (matmul(mirror_ref[:, opposite], flip) * gain).astype(BF16)
+        square = own * own
+        square = square[:, :128] + square[:, 128:]
+        squares = square if squares is None else squares + square
 
     @pl.when(pl.program_id(0) == 0)
     def _():
-        squares_ref[...] = jnp.zeros_like(squares_ref)
-
-    square = own * own
-    squares_ref[...] += square[:, :128] + square[:, 128:]
+        squares_ref[...] = squares
+
+    @pl.when(pl.program_id(0) > 0)
+    def _():
+        squares_ref[...] += squares
 
 
 def prepare(hidden, gain):
     length, depth = hidden.shape
-    count = depth // COLS
+    span = 4 * COLS
+    count = depth // span
     return pl.pallas_call(
         prepare_kernel,
         grid=(count,),
         in_specs=[
-            pl.BlockSpec((length, COLS), lambda j: (0, j)),
-            pl.BlockSpec((length, COLS), lambda j: (0, count - 1 - j)),
-            pl.BlockSpec((1, COLS), lambda j: (0, j)),
+            pl.BlockSpec((length, span), lambda j: (0, j)),
+            pl.BlockSpec((length, span), lambda j: (0, count - 1 - j)),
+            pl.BlockSpec((1, span), lambda j: (0, j)),
         ],
         out_specs=[
-            pl.BlockSpec((2, length, COLS), lambda j: (0, 0, j)),
+            pl.BlockSpec((2, length, span), lambda j: (0, 0, j)),
             pl.BlockSpec((length, 128), lambda j: (0, 0)),
         ],
         out_shape=[
@@ -292,60 +304,66 @@
     width = COLS // heads
     row = lax.broadcasted_iota(jnp.int32, (ROWS, ROWS), 0)
     col = lax.broadcasted_iota(jnp.int32, (ROWS, ROWS), 1)
-    left = (lax.broadcasted_iota(jnp.int32, (1, 2 * width), 1) < width).astype(F32).astype(BF16)
-    right = (1.0 - left.astype(F32)).astype(BF16)
+    on_left = lax.broadcasted_iota(jnp.int32, (1, 2 * width), 1) < width
+    left = on_left.astype(F32).astype(BF16)
+    right = (1.0 - on_left.astype(F32)).astype(BF16)
     blocks = length // ROWS
+
+    def diagonal(pair):
+        return jnp.concatenate([pair * left, pair * right], axis=0)
+
     for d in range(2):
-        carried = jnp.zeros((state, COLS), F32)
+        carried = [None] * (heads // 2)
         reach = (row >= col) if d == 0 else (row <= col)
         order = range(blocks) if d == 0 else range(blocks - 1, -1, -1)
         for lap, i in enumerate(order):
             own = slice(i * ROWS, (i + 1) * ROWS)
-            aux = aux_ref[0, 0, own]
-            cum = aux[:, d * heads : (d + 1) * heads]
-            steps = aux[:, 2 * heads :]
-            x = x_ref[0, d, own].astype(F32)
-            xd = x * spread(steps, width)
-            xd16 = xd.astype(BF16)
+            cum = aux_ref[0, 0, own, d * heads : (d + 1) * heads]
+            lines = row_ref[0, 0, d * heads : (d + 1) * heads, own]
             c_rows = bc_ref[0, d, own, state:]
+            c_wide = c_rows.astype(F32)
+            b_wide = bt_ref[0, d, :, own].astype(F32)
             scores = lax.dot_general(
                 c_rows, bc_ref[0, d, own, :state], (((1,), (1,)), ((), ())),
                 preferred_element_type=F32,
             )
-            scores = jnp.where(reach, scores, 0.0)
-            parts = []
-            for p in range(heads // 2):
-                weights = []
-                for h in (2 * p, 2 * p + 1):
-                    line = row_ref[0, 0, d * heads + h : d * heads + h + 1, own]
-                    gap = jnp.minimum(cum[:, h : h + 1] - line, 0.0)
-                    weights.append((jnp.exp(gap) * scores).astype(BF16))
-                both = xd16[:, 2 * p * width : 2 * (p + 1) * width]
-                stacked = jnp.concatenate([both * left, both * right], axis=0)
-                parts.append(matmul(jnp.concatenate(weights, axis=1), stacked))
-            local = jnp.concatenate(parts, axis=1)
+            final = cum[ROWS - 1 :] if d == 0 else cum[:1]
             if lap > 0:
                 entry = (i * ROWS - 1) if d == 0 else (i + 1) * ROWS
                 base = aux_ref[0, 0, entry : entry + 1, d * heads : (d + 1) * heads]
-                local = local + spread(jnp.exp(cum - base), width) * matmul(
-                    c_rows, carried.astype(BF16)
-                )
-            else:
-                base = jnp.zeros((1, heads), F32)
-            local = local + skip_ref[...] * x
-            if d == 0:
-                y_ref[0, own] = local
-            else:
-                y_ref[0, own] += local
-            if lap < blocks - 1:
-                last = cum[ROWS - 1 :] if d == 0 else cum[:1]
-                tail = spread(jnp.exp(last - cum), width)
-                fresh = matmul(bt_ref[0, d, :, own], (xd * tail).astype(BF16))
-                if lap > 0:
-                    decay = spread(jnp.broadcast_to(jnp.exp(last - base), (8, heads)), width)
-                    carried = decay[:1] * carried + fresh
+            for p in range(heads // 2):
+                weights, tails, entries, decays = [], [], [], []
+                for h in (2 * p, 2 * p + 1):
+                    tall = jnp.broadcast_to(cum[:, h : h + 1], (ROWS, ROWS))
+                    line = lines[h : h + 1]
+                    gap = jnp.where(reach, tall - line, -jnp.inf)
+                    weights.append((jnp.exp(gap) * scores).astype(BF16))
+                    if lap < blocks - 1:
+                        tails.append((b_wide * jnp.exp(final[:, h : h + 1] - line)).astype(BF16))
+                    if lap > 0:
+                        start = base[:, h : h + 1]
+                        entries.append((c_wide * jnp.exp(tall - start)).astype(BF16))
+                        decays.append(jnp.exp(final[:, h : h + 1] - start))
+                at = slice(2 * p * width, 2 * (p + 1) * width)
+                x = x_ref[0, d, own, at]
+                lhs = jnp.concatenate(weights, axis=1)
+                if tails:
+                    lhs = jnp.concatenate([lhs, jnp.concatenate(tails, axis=1)], axis=0)
+                result = matmul(lhs, diagonal(x))
+                local = result[:ROWS] + skip_ref[:, at] * x.astype(F32)
+                if entries:
+                    local = local + matmul(
+                        jnp.concatenate(entries, axis=1), diagonal(carried[p].astype(BF16))
+                    )
+                if tails:
+                    fresh = result[ROWS:]
+                    if entries:
+                        fresh = jnp.where(on_left, decays[0], decays[1]) * carried[p] + fresh
+                    carried[p] = fresh
+                if d == 0:
+                    y_ref[0, own, at] = local
                 else:
-                    carried = fresh
+                    y_ref[0, own, at] += local
     pl.when(step == last_step)(end)
 
 
@@ -417,8 +435,8 @@
         same = square if same is None else same | square
     same = same.astype(F32).astype(BF16)
     length = y_ref.shape[1]
-    for start in range(0, length, ROWS):
-        own = slice(start, start + ROWS)
+    for start in range(0, length, 2 * ROWS):
+        own = slice(start, start + 2 * ROWS)
         aux = aux_ref[0, 0, own]
         y = y_ref[0, own]
         for d in range(2):
@@ -604,7 +622,8 @@
     packed = jnp.concatenate([cum, steps[:, None]], axis=1)
     packed = packed.reshape(2, 3, length, chunks, per)
     aux = packed.transpose(0, 3, 2, 1, 4).reshape(2, chunks, length, 3 * per)
-    rows = packed[:, :2].transpose(0, 3, 1, 4, 2).reshape(2, chunks, 2 * per, length)
+    lines = (cum - jnp.log(steps)[:, None]).reshape(2, 2, length, chunks, per)
+    rows = lines.transpose(0, 3, 1, 4, 2).reshape(2, chunks, 2 * per, length)
 
     x, bc, bt, local = mix(value_in, bc_in, before, after, conv_value, conv_bc, aux, keep)
     total = jnp.broadcast_to(jnp.repeat(log_total, width, axis=-1)[:, None], (2, 8, inner))

time: 192 us -> 180 us (0.938); the launches traced: 189 us -> 179 us
  Pallas kernels: 131 us -> 123 us
    pallas_call x1, Pallas kernels: 49.7 us -> 43.1 us  [scan_local(): pl.pallas_call(functools.partial(scan_kernel, size), grid=(2, chunks), in...]
    pallas_call x1, Pallas kernels: 33.7 us -> 38.4 us  [project_out(): pl.pallas_call(functools.partial(project_out_kernel, count), in_specs=[pl...]
    pallas_call x1, Pallas kernels: 14 us -> 9.38 us  [prepare(): pl.pallas_call(prepare_kernel, grid=(count,), in_specs=[pl.BlockSpec((len...]
where the time goes in v3:
time: 180 us; the launch traced here: 179 us
  Pallas kernels  123 us (68%)
  matrix products  37.1 us (21%)
  local copies, waits for them, and re-layouts  13.9 us (8%)
  starting transfers between devices  3.66 us (2%)
    pallas_call x1, Pallas kernels, scan_local(): pl.pallas_call(functools.partial(scan_kernel, size), grid=(2, chunks), in...  43.1 us
    pallas_call x1, Pallas kernels, project_out(): pl.pallas_call(functools.partial(project_out_kernel, count), in_specs=[pl...  38.4 us
    dot_general x4, matrix products, project(): jnp.einsum('btd,dk->btk', scaled, weight, preferred_element_type=F32)  35 us
    pallas_call x1, Pallas kernels, mix(): pl.pallas_call(mix_kernel, grid=(2, chunks + 1), in_specs=[pl.BlockSpec((...  20.8 us
    pallas_call x1, Pallas kernels, finish(): pl.pallas_call(finish_kernel, grid=(2, chunks), in_specs=[pl.BlockSpec((1...  11 us
    pallas_call x1, Pallas kernels, prepare(): pl.pallas_call(prepare_kernel, grid=(count,), in_specs=[pl.BlockSpec((len...  9.38 us
    unnamed x25, local copies, waits for them, and re-layouts  6 us
  transfers between devices with their start and end apart: 2, of which 0 were waited for; matrix products, arithmetic and copies ran while one was open for 14% of the time, Pallas kernels for 0%

profile of v3, /device:TPU:0, one launch (start us, length us, event | category | flops | bytes accessed | tf_op | source)
XLA Modules:
  0.0 179.0 jit_solution(3089323891116146773)
XLA Ops:
  0.0 0.0 copy-start
  0.0 9.4 %prepare.1 = (bf16[2,512,4096]{2,1,0:T(8,128)(2,1)}, f32[512,128]{1,0:T(8,128)}) custom-call(bf16[512,4096]{1,0:T(8,128)(2,1)} %mirror_ref.1, bf16[512,4096]{1,0:T(8,128)(2,1)} %mirror_ref.1, f32[1,4096]{1,0:T(1,128)} %bitcast.63), custom_call_target="tpu_custom_call" | custom-call | tf_op jit(solution)/shard_map/prepare/pallas_call | solution.py:80
  9.4 1.1 reduce_sum.9
  10.5 0.0 copy-done
  10.5 0.0 copy-start.4
  10.5 5.9 %fusion.15.bc_ref = f32[2,512,256]{2,1,0:T(8,128)S(1)} fusion(bf16[2,512,4096]{2,1,0:T(8,128)(2,1)} %get-tuple-element.13, bf16[4096,256]{1,0:T(8,128)(2,1)S(1)} %copy-done, f32[512]{0:T(512)S(1)} %add_rsqrt_fusion), kind=kOutput, calls=%fused_computation.12 | convolution fusion | flops 2147745792 | bytes 11536384 | tf_op jit(solution)/shard_map/btd,dk->btk/dot_general | solution.py:601
  16.4 0.0 copy-start.6
  16.4 0.0 copy-done.4
  16.4 0.0 copy-start.11
  16.4 0.0 copy-start.7
  16.4 0.0 copy-start.8
  16.5 11.6 %fusion.4.v_ref = f32[2,512,1024]{2,1,0:T(8,128)S(1)} fusion(bf16[2,512,4096]{2,1,0:T(8,128)(2,1)S(1)} %copy-done.4, bf16[4096,1024]{1,0:T(8,128)(2,1)} %param.18, f32[512]{0:T(512)S(1)} %add_rsqrt_fusion), kind=kOutput, calls=%fused_computation.4 | convolution fusion | flops 8590983168 | bytes 20973568 | tf_op jit(solution)/shard_map/btd,dk->btk/dot_general | solution.py:601
  28.1 0.0 copy-done.6
  28.1 0.0 copy-start.5
  28.1 2.4 %collective-permute-start = (f32[2,8,1280]{2,1,0:T(8,128)S(1)}, f32[2,8,1280]{2,1,0:T(8,128)S(1)}, u32[]{:S(2)}, u32[]{:S(2)}) collective-permute-start(f32[2,8,1280]{2,1,0:T(8,128)S(1)} %pad_maximum_fusion.1), channel_id=1, source_target_pairs={{0,4},{4,8},{8,12},{12,16},{16,20},{20,24},{24,28},{1,5},{5,9},{9,... | collective-permute-start | bytes 245768 | tf_op jit(solution)/shard_map/ppermute | solution.py:612
  30.5 1.3 collective-permute-start.1
  31.8 0.1 fusion.20
  32.0 0.0 copy-done.11
  32.0 0.0 copy-start.9
  32.0 0.0 copy-start.10
  32.0 2.3 %fusion.31 = (f32[2,512,16]{1,2,0:T(8,128)S(1)}, f32[2,512,16]{1,2,0:T(8,128)S(1)}) fusion(f32[16]{0:T(128)S(1)} %copy-done.8, f32[512]{0:T(512)S(1)} %add_rsqrt_fusion, bf16[2,512,4096]{2,1,0:T(8,128)(2,1)S(1)} %copy-done.4, bf16[4096,16]{0,1:T(8,128)(2,1)S(1)} %copy-done.7), kind=kOutput, calls=%fused_computation.36 | convolution fusion | flops 134348800 | bytes 8652864 | tf_op jit(solution)/shard_map/btd,dk->btk/dot_general | solution.py:601
  34.4 2.1 %broadcast_subtract_fusion = (f32[2,2,512,16]{2,3,1,0:T(8,128)S(1)}, f32[2,2,512,16]{2,3,1,0:T(8,128)S(1)}) fusion(f32[2,512,16]{1,2,0:T(8,128)S(1)} %get-tuple-element.25, f32[1,512,512]{2,1,0:T(8,128)S(1)} %get-tuple-element.30, f32[1,512,512]{2,1,0:T(8,128)S(1)} %get-tuple-element.29, f32[2,512,16]{1,2,0:T(8,128)S(1)} %get-tuple-element.26, f32[16]{0:T(128)S(1)} %neg.7), kind=kOutput, calls=%fused_computation.27 | convolution fusion | flops 201900032 | bytes 2490432 | tf_op jit(solution)/shard_map/dts,bsh->bdth/dot_general | solution.py:620
  36.4 0.2 slice_reduce_fusion
  36.7 0.1 broadcast_in_dim.40
  36.7 0.7 broadcast_in_dim_reshape.4.skip_ref
  37.4 0.9 copy.21.keep_ref
  38.3 0.7 reshape.52.row_ref
  39.1 0.1 copy.18
  39.1 0.1 broadcast_in_dim.41
  39.2 0.1 broadcast_in_dim.42
  39.3 15.2 %fusion.7.gate_ref = f32[2,512,1024]{2,1,0:T(8,128)} fusion(bf16[2,512,4096]{2,1,0:T(8,128)(2,1)} %get-tuple-element.13, bf16[4096,1024]{1,0:T(8,128)(2,1)} %param.17, f32[512]{0:T(512)S(1)} %add_rsqrt_fusion), kind=kOutput, calls=%fused_computation.5 | convolution fusion | flops 8590983168 | bytes 20973568 | tf_op jit(solution)/shard_map/btd,dk->btk/dot_general | solution.py:601
  54.6 2.0 %copy.20.aux_ref = f32[2,4,512,12]{3,2,1,0:T(8,128)} copy(f32[2,4,512,12]{2,1,3,0:T(4,128)S(1)} %bitcast.61) | data formatting | bytes 393216 | tf_op jit(solution)/shard_map/reshape | solution.py:624
  56.5 0.0 collective-permute-done
  56.5 0.6 slice.39.before_bc
  57.1 0.6 slice.38.before_v
  57.8 0.0 collective-permute-done.1
  57.8 0.6 slice.43.after_bc
  58.4 0.6 slice.42.after_v
  59.0 20.8 %mix.1 = (bf16[2,2,512,1024]{3,2,1,0:T(8,128)(2,1)}, bf16[2,2,512,256]{3,2,1,0:T(8,128)(2,1)}, bf16[2,2,128,512]{3,2,1,0:T(8,128)(2,1)}, f32[2,2,128,1024]{3,2,1,0:T(8,128)}) custom-call(f32[2,512,1024]{2,1,0:T(8,128)} %copy-done.5, f32[2,512,256]{2,1,0:T(8,128)} %copy-done.6, f32[2,8,1024]{2,1,0:T(8,128)} %slice.38.before_v, f32[2,8,256]{2,1,0:T(8,128)} %slice.39.before_bc, ...), custom_call_target="tpu_custom_call" | custom-call | flops 536870912 | bytes 14680064 | tf_op jit(solution)/shard_map/mix/pallas_call | solution.py:165
  79.8 0.6 broadcast_in_dim.43.total_ref
  80.5 43.1 %scan_local.1 = (f32[2,512,1024]{2,1,0:T(8,128)}, bf16[2,2,128,1024]{3,2,1,0:T(8,128)(2,1)}) custom-call(bf16[2,2,512,1024]{3,2,1,0:T(8,128)(2,1)} %get-tuple-element.15.x_ref, bf16[2,2,512,256]{3,2,1,0:T(8,128)(2,1)} %get-tuple-element.16.bc_ref, bf16[2,2,128,512]{3,2,1,0:T(8,128)(2,1)} %get-tuple-element.17.bt_ref, f32[2,4,512,12]{3,2,1,0:T(8,128)} %copy.20.aux_ref, ...), custom_call_target="tpu_custom_call" | custom-call | flops 8589934592 | bytes 10485760 | tf_op jit(solution)/shard_map/scan_local/pallas_call | solution.py:378
  123.6 0.0 copy-start.1
  123.6 11.0 %finish.1.normed_ref = bf16[2,512,1024]{2,1,0:T(8,128)(2,1)} custom-call(f32[2,512,1024]{2,1,0:T(8,128)} %get-tuple-element.19.y_ref, bf16[2,2,512,256]{3,2,1,0:T(8,128)(2,1)} %get-tuple-element.16.bc_ref, bf16[2,2,128,1024]{3,2,1,0:T(8,128)(2,1)} %get-tuple-element.20.s_ref, f32[2,4,512,12]{3,2,1,0:T(8,128)} %copy.20.aux_ref, ...), custom_call_target="tpu_custom_call" | custom-call | tf_op jit(solution)/shard_map/finish/pallas_call | solution.py:454
  134.6 3.4 %copy-done.2 = bf16[1024,4096]{1,0:T(8,128)(2,1)S(1)} copy-done((bf16[1024,4096]{1,0:T(8,128)(2,1)S(1)}, bf16[1024,4096]{1,0:T(8,128)(2,1)}, u32[]{:S(2)}) %copy-start.2) | copy-done | bytes 8388632
  138.0 1.6 copy-done.3
  139.6 38.4 %project_out.1 = bf16[512,1024]{1,0:T(8,128)(2,1)S(1)} custom-call(bf16[2,512,1024]{2,1,0:T(8,128)(2,1)S(1)} %copy-done.3, bf16[1024,4096]{1,0:T(8,128)(2,1)S(1)} %copy-done.2), custom_call_target="tpu_custom_call" | custom-call | tf_op jit(solution)/shard_map/project_out/pallas_call | solution.py:566
  178.1 1.0 copy.29
  179.0 0.0 copy-done.1
  (20 shorter events, 0.2 us)
Async XLA Ops:
  0.0 10.5 %copy-start = (bf16[4096,256]{1,0:T(8,128)(2,1)S(1)}, bf16[4096,256]{1,0:T(8,128)(2,1)}, u32[]{:S(2)}) copy-start(bf16[4096,256]{1,0:T(8,128)(2,1)} %param.19) | copy-start | bytes 6291460
  10.5 5.9 %copy-start.4 = (bf16[2,512,4096]{2,1,0:T(8,128)(2,1)S(1)}, bf16[2,512,4096]{2,1,0:T(8,128)(2,1)}, u32[]{:S(2)}) copy-start(bf16[2,512,4096]{2,1,0:T(8,128)(2,1)} %get-tuple-element.13) | copy-start | bytes 25165828
  16.4 11.7 %copy-start.6 = (f32[2,512,256]{2,1,0:T(8,128)}, f32[2,512,256]{2,1,0:T(8,128)S(1)}, u32[]{:S(2)}) copy-start(f32[2,512,256]{2,1,0:T(8,128)S(1)} %fusion.15.bc_ref) | copy-start | bytes 3145732
  16.4 15.5 %copy-start.11 = (f32[16]{0:T(128)S(1)}, f32[16]{0:T(128)}, u32[]{:S(2)}) copy-start(f32[16]{0:T(128)} %param.24) | copy-start | bytes 196
  16.4 15.5 %copy-start.7 = (bf16[4096,16]{0,1:T(8,128)(2,1)S(1)}, bf16[4096,16]{0,1:T(8,128)(2,1)}, u32[]{:S(2)}) copy-start(bf16[4096,16]{0,1:T(8,128)(2,1)} %param.20) | copy-start | bytes 393220
  16.4 15.5 %copy-start.8 = (f32[16]{0:T(128)S(1)}, f32[16]{0:T(128)}, u32[]{:S(2)}) copy-start(f32[16]{0:T(128)} %param.23) | copy-start | bytes 196
  28.1 6.3 %copy-start.5 = (f32[2,512,1024]{2,1,0:T(8,128)}, f32[2,512,1024]{2,1,0:T(8,128)S(1)}, u32[]{:S(2)}) copy-start(f32[2,512,1024]{2,1,0:T(8,128)S(1)} %fusion.4.v_ref) | copy-start | bytes 12582916
  28.1 28.4 %collective-permute-start = (f32[2,8,1280]{2,1,0:T(8,128)S(1)}, f32[2,8,1280]{2,1,0:T(8,128)S(1)}, u32[]{:S(2)}, u32[]{:S(2)}) collective-permute-start(f32[2,8,1280]{2,1,0:T(8,128)S(1)} %pad_maximum_fusion.1), channel_id=1, source_target_pairs={{0,4},{4,8},{8,12},{12,16},{16,20},{20,24},{24,28},{1,5},{5,9},{9,... | collective-permute-start | bytes 245768 | tf_op jit(solution)/shard_map/ppermute | solution.py:612
  30.5 27.3 %collective-permute-start.1 = (f32[2,8,1280]{2,1,0:T(8,128)S(1)}, f32[2,8,1280]{2,1,0:T(8,128)S(1)}, u32[]{:S(2)}, u32[]{:S(2)}) collective-permute-start(f32[2,8,1280]{2,1,0:T(8,128)S(1)} %pad_maximum_fusion.2), channel_id=1, source_target_pairs={{4,0},{8,4},{12,8},{16,12},{20,16},{24,20},{28,24},{5,1},{9,5},{13... | collective-permute-start | bytes 245768 | tf_op jit(solution)/shard_map/ppermute | solution.py:613
  32.0 4.7 %copy-start.9 = (s32[512]{0:T(512)S(1)}, s32[512]{0:T(512)}, u32[]{:S(2)}) copy-start(s32[512]{0:T(512)} %param.15) | copy-start | bytes 6148
  32.0 4.7 %copy-start.10 = (f32[16]{0:T(128)S(1)}, f32[16]{0:T(128)}, u32[]{:S(2)}) copy-start(f32[16]{0:T(128)} %param.25) | copy-start | bytes 196
  123.6 55.5 %copy-start.1 = (bf16[4096,256]{1,0:T(8,128)(2,1)S(1)}, bf16[4096,256]{1,0:T(8,128)(2,1)}, u32[]{:S(2)}) copy-start(bf16[4096,256]{1,0:T(8,128)(2,1)} %param.19) | copy-start | bytes 6291460
  134.6 3.4 %copy-start.2 = (bf16[1024,4096]{1,0:T(8,128)(2,1)S(1)}, bf16[1024,4096]{1,0:T(8,128)(2,1)}, u32[]{:S(2)}) copy-start(bf16[1024,4096]{1,0:T(8,128)(2,1)} %w_ref.1) | copy-start | bytes 25165828
  138.0 1.6 copy-start.3

commit v4 on v3

--- a/solution.py
+++ b/solution.py
@@ -14,12 +14,12 @@
 COLS = 256
 ROWS = 128
 HALO = 8
-VMEM_LIMIT = 56 * 1024 * 1024
-
-
-def params(dims):
+MIB = 1024 * 1024
+
+
+def params(dims, mib):
     return pltpu.CompilerParams(
-        vmem_limit_bytes=VMEM_LIMIT, dimension_semantics=("arbitrary",) * dims
+        vmem_limit_bytes=mib * MIB, dimension_semantics=("arbitrary",) * dims
     )
 
 
@@ -93,7 +93,7 @@
             jax.ShapeDtypeStruct((2, length, depth), BF16),
             jax.ShapeDtypeStruct((length, 128), F32),
         ],
-        compiler_params=params(1),
+        compiler_params=params(1, 20),
         name="prepare",
     )(hidden, hidden, gain[None])
 
@@ -190,7 +190,7 @@
             jax.ShapeDtypeStruct((2, 2, state, inner), F32),
         ],
         scratch_shapes=[pltpu.VMEM((length + 2 * HALO, COLS), F32)],
-        compiler_params=params(2),
+        compiler_params=params(2, 16),
         cost_estimate=pl.CostEstimate(
             flops=2 * 4 * length * state * inner,
             bytes_accessed=14 * 2 * length * inner,
@@ -204,12 +204,12 @@
           hop_out, hop_in, crossed, send_sems, recv_sems):
     me = lax.axis_index("ctx")
     odd = lax.rem(me, 2)
-    hops = size // 2 - 1
     ahead = me + 4 * odd - 2
     behind = me - 4 * odd + 2
     has_ahead = (ahead >= 0) & (ahead < size)
     has_behind = (behind >= 0) & (behind < size)
     partner = me + 1 - 2 * odd
+    place = me // 2 * (2 * odd - 1) + (1 - odd) * (size // 2 - 1)
 
     def remote(source, target, index, device):
         return pltpu.make_async_remote_copy(
@@ -223,8 +223,8 @@
 
     swap_copy = remote(kept, swapped, 0, partner)
     decay_copy = remote(total_ref, decay_other, 1, partner)
-    cross_copy = remote(kept, crossed, 2, partner)
-    hop_copies = [remote(hop_out.at[k], hop_in.at[k], 3 + k, ahead) for k in range(hops)]
+    cross_copies = [remote(kept.at[b], crossed.at[b], 2 + b, partner) for b in range(2)]
+    hop_copies = [remote(hop_out.at[b], hop_in.at[b], 4 + b, ahead) for b in range(2)]
 
     def greet():
         barrier = pltpu.get_barrier_semaphore()
@@ -255,40 +255,31 @@
             mine = jnp.where(odd == 1, local_ref[b, 0], local_ref[b, 1])
             decay = jnp.exp(total_ref[b, :1])
             chip[b] = decay * swapped[b].astype(F32) + mine
-            hop_out[0, b] = chip[b].astype(BF16)
-        pl.when(has_ahead)(lambda: hop_copies[0].start())
-
-    def entered(k, b):
-        return jnp.where(has_behind, hop_in[k, b].astype(F32), 0.0)
-
-    def hop(k):
+
+    def link(b):
         def stage():
-            pl.when(has_behind)(lambda: hop_copies[k - 1].wait_recv())
-            for b in range(2):
-                decay = jnp.exp(total_ref[b, :1] + decay_other[b, :1])
-                hop_out[k, b] = (chip[b] + decay * entered(k - 1, b)).astype(BF16)
-            pl.when(has_ahead)(lambda: hop_copies[k].start())
+            pl.when(has_behind)(lambda: hop_copies[b].wait_recv())
+            decay = jnp.exp(total_ref[b, :1] + decay_other[b, :1])
+            entering = jnp.where(has_behind, hop_in[b].astype(F32), 0.0)
+            hop_out[b] = (chip[b] + decay * entering).astype(BF16)
+            pl.when(has_ahead)(lambda: hop_copies[b].start())
+            kept[b] = entering.astype(BF16)
+            cross_copies[b].start()
 
         return stage
 
-    def cross():
-        pl.when(has_behind)(lambda: hop_copies[hops - 1].wait_recv())
+    def end():
         for b in range(2):
-            kept[b] = entered(hops - 1, b).astype(BF16)
-        cross_copy.start()
-
-    def end():
-        cross_copy.wait()
-        for b in range(2):
+            cross_copies[b].wait()
             own = jnp.exp(decay_other[b, :1]) * kept[b].astype(F32) + swapped[b].astype(F32)
             other = crossed[b].astype(F32)
             ent_ref[b, 0] = jnp.where(odd == 1, own, other).astype(BF16)
             ent_ref[b, 1] = jnp.where(odd == 1, other, own).astype(BF16)
-        for k in range(hops):
-            pl.when(has_ahead)(lambda k=k: hop_copies[k].wait_send())
-
-    stages = [first, second] + [hop(k) for k in range(1, hops)] + [cross]
-    return [(min(last, (7 * i) // 5), stage) for i, stage in enumerate(stages)], end
+            pl.when(has_ahead)(lambda b=b: hop_copies[b].wait_send())
+
+    stages = [(0, first), (1, second)]
+    stages += [(jnp.minimum(place + b + 1, last), link(b)) for b in range(2)]
+    return stages, end
 
 
 def scan_kernel(size, x_ref, bc_ref, bt_ref, aux_ref, row_ref, skip_ref, local_ref, total_ref,
@@ -369,7 +360,6 @@
 
 def scan_local(x, bc, bt, aux, rows, skip, local, total):
     size = lax.axis_size("ctx")
-    hops = size // 2 - 1
     wide = local.shape[2:]
     _, _, length, inner = x.shape
     pair = bc.shape[3]
@@ -401,14 +391,14 @@
             pltpu.VMEM(total.shape, F32),
             pltpu.VMEM((2,) + wide, F32),
             pltpu.VMEM((2,) + wide, BF16),
-            pltpu.VMEM((hops, 2) + wide, BF16),
-            pltpu.VMEM((hops, 2) + wide, BF16),
             pltpu.VMEM((2,) + wide, BF16),
-            pltpu.SemaphoreType.DMA((3 + hops,)),
-            pltpu.SemaphoreType.DMA((3 + hops,)),
+            pltpu.VMEM((2,) + wide, BF16),
+            pltpu.VMEM((2,) + wide, BF16),
+            pltpu.SemaphoreType.DMA((6,)),
+            pltpu.SemaphoreType.DMA((6,)),
         ],
         compiler_params=pltpu.CompilerParams(
-            vmem_limit_bytes=VMEM_LIMIT,
+            vmem_limit_bytes=28 * MIB,
             dimension_semantics=("arbitrary",) * 2,
             collective_id=1,
             has_side_effects=True,
@@ -464,7 +454,7 @@
         ],
         out_specs=pl.BlockSpec((1, length, COLS), lambda b, c: (b, 0, c)),
         out_shape=jax.ShapeDtypeStruct((2, length, inner), BF16),
-        compiler_params=params(2),
+        compiler_params=params(2, 12),
         name="finish",
     )(y, bc, entering, aux, gate_in, gain)
 
@@ -576,7 +566,7 @@
             pltpu.SemaphoreType.DMA((slots,)),
         ],
         compiler_params=pltpu.CompilerParams(
-            vmem_limit_bytes=40 * 1024 * 1024, collective_id=0, has_side_effects=True
+            vmem_limit_bytes=28 * MIB, collective_id=0, has_side_effects=True
         ),
         name="project_out",
     )(normed, w_out)

time: 180 us -> 167 us (0.928)
  Pallas kernels: 123 us -> 102 us
  local copies, waits for them, and re-layouts: 13.9 us -> 20.1 us
    pallas_call x1, Pallas kernels: 43.1 us -> 33.5 us  [scan_local(): pl.pallas_call(functools.partial(scan_kernel, size), grid=(2, chunks), in...]
    unnamed x25 -> x49, local copies, waits for them, and re-layouts: 6 us -> 11.8 us
    pallas_call x1, Pallas kernels: 9.38 us -> 4.88 us  [prepare(): pl.pallas_call(prepare_kernel, grid=(count,), in_specs=[pl.BlockSpec((len...]
    pallas_call x1, Pallas kernels: 11 us -> 7.29 us  [finish(): pl.pallas_call(finish_kernel, grid=(2, chunks), in_specs=[pl.BlockSpec((1...]
    pallas_call x1, Pallas kernels: 20.8 us -> 18.7 us  [mix(): pl.pallas_call(mix_kernel, grid=(2, chunks + 1), in_specs=[pl.BlockSpec((...]
  transfers between devices with their start and end apart: 2 -> 2, of which waited for: 0 -> 0; matrix products, arithmetic and copies ran while one was open for 14% -> 17% of each run, Pallas kernels for 0% -> 0%
where the time goes in v4:
time: 167 us; the launch traced here: 166 us
  Pallas kernels  102 us (61%)
  matrix products  36.5 us (22%)
  local copies, waits for them, and re-layouts  20.1 us (12%)
  starting transfers between devices  4.26 us (3%)
  other arithmetic  2.45 us (1%)
    pallas_call x1, Pallas kernels, project_out(): pl.pallas_call(functools.partial(project_out_kernel, count), in_specs=[pl...  38.1 us
    dot_general x4, matrix products, project(): jnp.einsum('btd,dk->btk', scaled, weight, preferred_element_type=F32)  34.5 us
    pallas_call x1, Pallas kernels, scan_local(): pl.pallas_call(functools.partial(scan_kernel, size), grid=(2, chunks), in...  33.5 us
    pallas_call x1, Pallas kernels, mix(): pl.pallas_call(mix_kernel, grid=(2, chunks + 1), in_specs=[pl.BlockSpec((...  18.7 us
    unnamed x49, local copies, waits for them, and re-layouts  11.8 us
    pallas_call x1, Pallas kernels, finish(): pl.pallas_call(finish_kernel, grid=(2, chunks), in_specs=[pl.BlockSpec((1...  7.29 us
    pallas_call x1, Pallas kernels, prepare(): pl.pallas_call(prepare_kernel, grid=(count,), in_specs=[pl.BlockSpec((len...  4.88 us
  transfers between devices with their start and end apart: 2, of which 0 were waited for; matrix products, arithmetic and copies ran while one was open for 17% of the time, Pallas kernels for 0%

profile of v4, /device:TPU:0, one launch (start us, length us, event | category | flops | bytes accessed | tf_op | source)
XLA Modules:
  0.0 166.3 jit_solution(9379603382701559657)
XLA Ops:
  0.0 2.3 %copy-done.6 = bf16[512,4096]{1,0:T(8,128)(2,1)S(1)} copy-done((bf16[512,4096]{1,0:T(8,128)(2,1)S(1)}, bf16[512,4096]{1,0:T(8,128)(2,1)}, u32[]{:S(2)}) %copy-start.6) | copy-done | bytes 4194328
  2.3 0.7 copy-done.10
  3.1 4.9 %prepare.1 = (bf16[2,512,4096]{2,1,0:T(8,128)(2,1)S(1)}, f32[512,128]{1,0:T(8,128)S(1)}) custom-call(bf16[512,4096]{1,0:T(8,128)(2,1)S(1)} %copy-done.6, bf16[512,4096]{1,0:T(8,128)(2,1)S(1)} %copy-done.6, f32[1,4096]{1,0:T(1,128)S(1)} %bitcast.63), custom_call_target="tpu_custom_call" | custom-call | tf_op jit(solution)/shard_map/prepare/pallas_call | solution.py:80
  7.9 0.0 copy-start.2
  8.0 3.3 %copy-done.2 = bf16[2,512,4096]{2,1,0:T(8,128)(2,1)} copy-done((bf16[2,512,4096]{2,1,0:T(8,128)(2,1)}, bf16[2,512,4096]{2,1,0:T(8,128)(2,1)S(1)}, u32[]{:S(2)}) %copy-start.2) | copy-done | bytes 8388632
  11.2 0.1 reduce_sum.9
  11.4 5.9 %fusion.15.bc_ref = f32[2,512,256]{2,1,0:T(8,128)S(1)} fusion(bf16[2,512,4096]{2,1,0:T(8,128)(2,1)} %copy-done.2, bf16[4096,256]{1,0:T(8,128)(2,1)S(1)} %copy-done, f32[512]{0:T(512)S(1)} %add_rsqrt_fusion), kind=kOutput, calls=%fused_computation.12 | convolution fusion | flops 2147745792 | bytes 11536384 | tf_op jit(solution)/shard_map/btd,dk->btk/dot_general | solution.py:591
  17.3 0.0 copy-start.21
  17.3 0.0 copy-start.16
  17.3 0.0 copy-start.18
  17.3 11.2 %fusion.4.v_ref = f32[2,512,1024]{2,1,0:T(8,128)S(1)} fusion(bf16[2,512,4096]{2,1,0:T(8,128)(2,1)S(1)} %copy-done.3, bf16[4096,1024]{1,0:T(8,128)(2,1)} %param.18, f32[512]{0:T(512)S(1)} %add_rsqrt_fusion), kind=kOutput, calls=%fused_computation.4 | convolution fusion | flops 8590983168 | bytes 20973568 | tf_op jit(solution)/shard_map/btd,dk->btk/dot_general | solution.py:591
  28.6 0.7 pad_maximum_fusion.1
  29.3 3.0 %collective-permute-start = (f32[2,8,1280]{2,1,0:T(8,128)}, f32[2,8,1280]{2,1,0:T(8,128)}, u32[]{:S(2)}, u32[]{:S(2)}) collective-permute-start(f32[2,8,1280]{2,1,0:T(8,128)} %pad_maximum_fusion.1), channel_id=1, source_target_pairs={{0,4},{4,8},{8,12},{12,16},{16,20},{20,24},{24,28},{1,5},{5,9},{9,... | collective-permute-start | bytes 245768 | tf_op jit(solution)/shard_map/ppermute | solution.py:602
  32.3 0.6 pad_maximum_fusion.2
  32.9 1.3 collective-permute-start.1
  34.2 0.2 fusion.20
  34.5 0.0 copy-start.19
  34.5 0.0 copy-start.20
  34.5 2.3 %fusion.31 = (f32[2,512,16]{1,2,0:T(8,128)S(1)}, f32[2,512,16]{1,2,0:T(8,128)S(1)}) fusion(f32[16]{0:T(128)S(1)} %copy-done.18, f32[512]{0:T(512)S(1)} %add_rsqrt_fusion, bf16[2,512,4096]{2,1,0:T(8,128)(2,1)S(1)} %copy-done.3, bf16[4096,16]{0,1:T(8,128)(2,1)S(1)} %copy-done.16), kind=kOutput, calls=%fused_computation.36 | convolution fusion | flops 134348800 | bytes 8652864 | tf_op jit(solution)/shard_map/btd,dk->btk/dot_general | solution.py:591
  36.9 0.7 concatenate.17
  37.5 2.1 %broadcast_subtract_fusion = (f32[2,2,512,16]{2,3,1,0:T(8,128)S(1)}, f32[2,2,512,16]{2,3,1,0:T(8,128)S(1)}) fusion(f32[2,512,16]{1,2,0:T(8,128)S(1)} %get-tuple-element.25, f32[1,512,512]{2,1,0:T(8,128)S(1)} %get-tuple-element.30, f32[1,512,512]{2,1,0:T(8,128)S(1)} %get-tuple-element.29, f32[2,512,16]{1,2,0:T(8,128)S(1)} %get-tuple-element.26, f32[16]{0:T(128)S(1)} %neg.7), kind=kOutput, calls=%fused_computation.27 | convolution fusion | flops 201900032 | bytes 2490432 | tf_op jit(solution)/shard_map/dts,bsh->bdth/dot_general | solution.py:610
  39.6 0.2 slice_reduce_fusion
  39.8 0.1 broadcast_in_dim.40
  39.9 0.7 broadcast_in_dim_reshape.4.skip_ref
  40.6 0.1 copy.21.keep_ref
  40.8 0.9 copy.19
  41.7 0.1 copy.18
  41.8 0.1 broadcast_in_dim.41
  41.8 0.7 broadcast_in_dim.42
  42.5 15.1 %fusion.7.gate_ref = f32[2,512,1024]{2,1,0:T(8,128)} fusion(bf16[2,512,4096]{2,1,0:T(8,128)(2,1)} %copy-done.2, bf16[4096,1024]{1,0:T(8,128)(2,1)} %param.17, f32[512]{0:T(512)} %copy-done.15), kind=kOutput, calls=%fused_computation.5 | convolution fusion | flops 8590983168 | bytes 20973568 | tf_op jit(solution)/shard_map/btd,dk->btk/dot_general | solution.py:591
  57.6 0.7 pad_maximum_fusion
  58.3 1.6 copy.20.aux_ref
  59.9 0.0 collective-permute-done
  59.9 0.8 slice.39.before_bc
  60.7 0.8 slice.38.before_v
  61.5 0.0 collective-permute-done.1
  61.5 0.7 slice.43.after_bc
  62.2 0.8 slice.42.after_v
  63.1 2.2 %copy-done.8 = f32[2,512,1024]{2,1,0:T(8,128)S(1)} copy-done((f32[2,512,1024]{2,1,0:T(8,128)S(1)}, f32[2,512,1024]{2,1,0:T(8,128)}, u32[]{:S(2)}) %copy-start.8) | copy-done | bytes 4194328
  65.3 0.7 copy-done.12
  66.0 18.7 %mix.1 = (bf16[2,2,512,1024]{3,2,1,0:T(8,128)(2,1)S(1)}, bf16[2,2,512,256]{3,2,1,0:T(8,128)(2,1)S(1)}, bf16[2,2,128,512]{3,2,1,0:T(8,128)(2,1)S(1)}, f32[2,2,128,1024]{3,2,1,0:T(8,128)S(1)}) custom-call(f32[2,512,1024]{2,1,0:T(8,128)S(1)} %copy-done.8, f32[2,512,256]{2,1,0:T(8,128)S(1)} %fusion.15.bc_ref, f32[2,8,1024]{2,1,0:T(8,128)S(1)} %slice.38.before_v, ...), custom_call_target="tpu_custom_call" | custom-call | flops 536870912 | bytes 14680064 | tf_op jit(solution)/shard_map/mix/pallas_call | solution.py:165
  84.7 0.0 copy-start.14
  84.8 0.0 slice-start.1
  84.8 33.5 %scan_local.1 = (f32[2,512,1024]{2,1,0:T(8,128)S(1)}, bf16[2,2,128,1024]{3,2,1,0:T(8,128)(2,1)S(1)}) custom-call(bf16[2,2,512,1024]{3,2,1,0:T(8,128)(2,1)S(1)} %get-tuple-element.15.x_ref, bf16[2,2,512,256]{3,2,1,0:T(8,128)(2,1)S(1)} %get-tuple-element.16.bc_ref, bf16[2,2,128,512]{3,2,1,0:T(8,128)(2,1)S(1)} %get-tuple-element.17.bt_ref, ...), custom_call_target="tpu_custom_call" | custom-call | flops 8589934592 | bytes 10485760 | tf_op jit(solution)/shard_map/scan_local/pallas_call | solution.py:368
  118.3 1.6 copy-done.5
  119.9 7.3 %finish.1.normed_ref = bf16[2,512,1024]{2,1,0:T(8,128)(2,1)S(1)} custom-call(f32[2,512,1024]{2,1,0:T(8,128)S(1)} %get-tuple-element.19.y_ref, bf16[2,2,512,256]{3,2,1,0:T(8,128)(2,1)S(1)} %get-tuple-element.16.bc_ref, bf16[2,2,128,1024]{3,2,1,0:T(8,128)(2,1)S(1)} %get-tuple-element.20.s_ref, f32[2,4,512,12]{3,2,1,0:T(8,128)S(1)} %copy-done.5, ...), custom_call_target="tpu_custom_call" | custom-call | tf_op jit(solution)/shard_map/finish/pallas_call | solution.py:444
  127.2 38.1 %project_out.1 = bf16[512,1024]{1,0:T(8,128)(2,1)S(1)} custom-call(bf16[2,512,1024]{2,1,0:T(8,128)(2,1)S(1)} %finish.1.normed_ref, bf16[1024,4096]{1,0:T(8,128)(2,1)S(1)} %bitcast.62), custom_call_target="tpu_custom_call" | custom-call | tf_op jit(solution)/shard_map/project_out/pallas_call | solution.py:556
  165.4 1.0 copy.29
  (45 shorter events, 0.2 us)
Async XLA Ops:
  0.0 11.4 %copy-start = (bf16[4096,256]{1,0:T(8,128)(2,1)S(1)}, bf16[4096,256]{1,0:T(8,128)(2,1)}, u32[]{:S(2)}) copy-start(bf16[4096,256]{1,0:T(8,128)(2,1)} %param.19) | copy-start | bytes 6291460
  0.0 2.3 %copy-start.6 = (bf16[512,4096]{1,0:T(8,128)(2,1)S(1)}, bf16[512,4096]{1,0:T(8,128)(2,1)}, u32[]{:S(2)}) copy-start(bf16[512,4096]{1,0:T(8,128)(2,1)} %mirror_ref.1) | copy-start | bytes 12582916
  2.3 0.7 copy-start.10
  7.9 3.3 %copy-start.2 = (bf16[2,512,4096]{2,1,0:T(8,128)(2,1)}, bf16[2,512,4096]{2,1,0:T(8,128)(2,1)S(1)}, u32[]{:S(2)}) copy-start(bf16[2,512,4096]{2,1,0:T(8,128)(2,1)S(1)} %get-tuple-element.13) | copy-start | bytes 25165828
  11.4 23.1 %copy-start.15 = (f32[512]{0:T(512)}, f32[512]{0:T(512)S(1)}, u32[]{:S(2)}) copy-start(f32[512]{0:T(512)S(1)} %add_rsqrt_fusion) | copy-start | bytes 6148
  11.4 5.9 %copy-start.3 = (bf16[2,512,4096]{2,1,0:T(8,128)(2,1)S(1)}, bf16[2,512,4096]{2,1,0:T(8,128)(2,1)}, u32[]{:S(2)}) copy-start(bf16[2,512,4096]{2,1,0:T(8,128)(2,1)} %copy-done.2) | copy-start | bytes 25165828
  17.3 17.2 %copy-start.21 = (f32[16]{0:T(128)S(1)}, f32[16]{0:T(128)}, u32[]{:S(2)}) copy-start(f32[16]{0:T(128)} %param.24) | copy-start | bytes 196
  17.3 17.2 %copy-start.16 = (bf16[4096,16]{0,1:T(8,128)(2,1)S(1)}, bf16[4096,16]{0,1:T(8,128)(2,1)}, u32[]{:S(2)}) copy-start(bf16[4096,16]{0,1:T(8,128)(2,1)} %param.20) | copy-start | bytes 393220
  17.3 17.2 %copy-start.18 = (f32[16]{0:T(128)S(1)}, f32[16]{0:T(128)}, u32[]{:S(2)}) copy-start(f32[16]{0:T(128)} %param.23) | copy-start | bytes 196
  28.6 8.3 %copy-start.7 = (f32[2,512,1024]{2,1,0:T(8,128)}, f32[2,512,1024]{2,1,0:T(8,128)S(1)}, u32[]{:S(2)}) copy-start(f32[2,512,1024]{2,1,0:T(8,128)S(1)} %fusion.4.v_ref) | copy-start | bytes 12582916
  29.3 30.6 %collective-permute-start = (f32[2,8,1280]{2,1,0:T(8,128)}, f32[2,8,1280]{2,1,0:T(8,128)}, u32[]{:S(2)}, u32[]{:S(2)}) collective-permute-start(f32[2,8,1280]{2,1,0:T(8,128)} %pad_maximum_fusion.1), channel_id=1, source_target_pairs={{0,4},{4,8},{8,12},{12,16},{16,20},{20,24},{24,28},{1,5},{5,9},{9,... | collective-permute-start | bytes 245768 | tf_op jit(solution)/shard_map/ppermute | solution.py:602
  32.9 28.6 %collective-permute-start.1 = (f32[2,8,1280]{2,1,0:T(8,128)}, f32[2,8,1280]{2,1,0:T(8,128)}, u32[]{:S(2)}, u32[]{:S(2)}) collective-permute-start(f32[2,8,1280]{2,1,0:T(8,128)} %pad_maximum_fusion.2), channel_id=1, source_target_pairs={{4,0},{8,4},{12,8},{16,12},{20,16},{24,20},{28,24},{5,1},{9,5},{13... | collective-permute-start | bytes 245768 | tf_op jit(solution)/shard_map/ppermute | solution.py:603
  34.5 5.3 %copy-start.19 = (s32[512]{0:T(512)S(1)}, s32[512]{0:T(512)}, u32[]{:S(2)}) copy-start(s32[512]{0:T(512)} %param.15) | copy-start | bytes 6148
  34.5 5.3 %copy-start.20 = (f32[16]{0:T(128)S(1)}, f32[16]{0:T(128)}, u32[]{:S(2)}) copy-start(f32[16]{0:T(128)} %param.25) | copy-start | bytes 196
  42.5 20.6 %copy-start.11 = (f32[4,1024]{1,0:T(4,128)S(1)}, f32[4,1024]{1,0:T(4,128)}, u32[]{:S(2)}) copy-start(f32[4,1024]{1,0:T(4,128)} %taps_v.1) | copy-start | bytes 49156
  59.9 58.4 %copy-start.4 = (f32[2,4,512,12]{3,2,1,0:T(8,128)}, f32[2,4,512,12]{3,2,1,0:T(8,128)S(1)}, u32[]{:S(2)}) copy-start(f32[2,4,512,12]{3,2,1,0:T(8,128)S(1)} %copy.20.aux_ref) | copy-start | bytes 589828
  59.9 24.8 %copy-start.17 = (f32[2,1024]{1,0:T(2,128)S(1)}, f32[2,1024]{1,0:T(2,128)}, u32[]{:S(2)}) copy-start(f32[2,1024]{1,0:T(2,128)} %broadcast_in_dim.42) | copy-start | bytes 24580
  59.9 24.8 %copy-start.13 = (f32[1,1024]{1,0:T(1,128)S(1)}, f32[1,1024]{1,0:T(1,128)}, u32[]{:S(2)}) copy-start(f32[1,1024]{1,0:T(1,128)} %broadcast_in_dim_reshape.4.skip_ref) | copy-start | bytes 12292
  63.1 2.2 %copy-start.8 = (f32[2,512,1024]{2,1,0:T(8,128)S(1)}, f32[2,512,1024]{2,1,0:T(8,128)}, u32[]{:S(2)}) copy-start(f32[2,512,1024]{2,1,0:T(8,128)} %copy-done.7) | copy-start | bytes 12582916
  65.3 0.7 copy-start.12
  66.0 61.2 %slice-start = ((s8[8388608]{0:T(1024)(128)(4,1)}), s8[4194304]{0:T(1024)(128)(4,1)S(1)}, s32[]{:S(2)}) async-start(s8[8388608]{0:T(1024)(128)(4,1)} %bitcast.61), calls=%async_computation | async-start | bytes 8388608
  84.7 33.5 %copy-start.9 = (f32[2,512,1024]{2,1,0:T(8,128)S(1)}, f32[2,512,1024]{2,1,0:T(8,128)}, u32[]{:S(2)}) copy-start(f32[2,512,1024]{2,1,0:T(8,128)} %fusion.7.gate_ref) | copy-start | bytes 12582916
  84.7 33.5 %copy-start.14 = (f32[1024]{0:T(1024)S(1)}, f32[1024]{0:T(1024)}, u32[]{:S(2)}) copy-start(f32[1024]{0:T(1024)} %param.26) | copy-start | bytes 12292
  84.8 42.4 %slice-start.1 = ((s8[8388608]{0:T(1024)(128)(4,1)}), s8[4194304]{0:T(1024)(128)(4,1)S(1)}, s32[]{:S(2)}) async-start(s8[8388608]{0:T(1024)(128)(4,1)} %bitcast.61), calls=%async_computation.1 | async-start | bytes 8388608
  118.3 1.6 copy-start.5
  119.9 46.4 %copy-start.1 = (bf16[4096,256]{1,0:T(8,128)(2,1)S(1)}, bf16[4096,256]{1,0:T(8,128)(2,1)}, u32[]{:S(2)}) copy-start(bf16[4096,256]{1,0:T(8,128)(2,1)} %param.19) | copy-start | bytes 6291460

commit v5 on v4

--- a/solution.py
+++ b/solution.py
@@ -49,7 +49,10 @@
     return half + half * jnp.tanh(half)
 
 
-def prepare_kernel(own_ref, mirror_ref, gain_ref, scaled_ref, squares_ref):
+def prepare_kernel(
+    depth, own_ref, mirror_ref, gain_ref, w_bc_ref, w_step_ref,
+    scaled_ref, bc_ref, step_ref, inv_ref, squares_ref,
+):
     flip = anti_identity(COLS)
     parts = own_ref.shape[1] // COLS
     squares = None
@@ -67,35 +70,58 @@
     @pl.when(pl.program_id(0) == 0)
     def _():
         squares_ref[...] = squares
+        for b in range(2):
+            bc_ref[b] = matmul(scaled_ref[b], w_bc_ref[...])
+            step_ref[b] = matmul(scaled_ref[b], w_step_ref[...])
 
     @pl.when(pl.program_id(0) > 0)
     def _():
         squares_ref[...] += squares
-
-
-def prepare(hidden, gain):
+        for b in range(2):
+            bc_ref[b] += matmul(scaled_ref[b], w_bc_ref[...])
+            step_ref[b] += matmul(scaled_ref[b], w_step_ref[...])
+
+    @pl.when(pl.program_id(0) == pl.num_programs(0) - 1)
+    def _():
+        total = jnp.sum(squares_ref[...], axis=1, keepdims=True)
+        inv = lax.rsqrt(total * (1.0 / depth) + EPSILON)
+        inv_ref[...] = inv
+        for b in range(2):
+            bc_ref[b] = bc_ref[b] * inv
+            step_ref[b] = step_ref[b] * inv
+
+
+def prepare(hidden, gain, w_bc, w_step):
     length, depth = hidden.shape
+    pair, heads = w_bc.shape[1], w_step.shape[1]
     span = 4 * COLS
     count = depth // span
     return pl.pallas_call(
-        prepare_kernel,
+        functools.partial(prepare_kernel, depth),
         grid=(count,),
         in_specs=[
             pl.BlockSpec((length, span), lambda j: (0, j)),
             pl.BlockSpec((length, span), lambda j: (0, count - 1 - j)),
             pl.BlockSpec((1, span), lambda j: (0, j)),
+            pl.BlockSpec((span, pair), lambda j: (j, 0)),
+            pl.BlockSpec((span, heads), lambda j: (j, 0)),
         ],
         out_specs=[
             pl.BlockSpec((2, length, span), lambda j: (0, 0, j)),
-            pl.BlockSpec((length, 128), lambda j: (0, 0)),
+            pl.BlockSpec((2, length, pair), lambda j: (0, 0, 0)),
+            pl.BlockSpec((2, length, heads), lambda j: (0, 0, 0)),
+            pl.BlockSpec((length, 1), lambda j: (0, 0)),
         ],
         out_shape=[
             jax.ShapeDtypeStruct((2, length, depth), BF16),
-            jax.ShapeDtypeStruct((length, 128), F32),
-        ],
+            jax.ShapeDtypeStruct((2, length, pair), F32),
+            jax.ShapeDtypeStruct((2, length, heads), F32),
+            jax.ShapeDtypeStruct((length, 1), F32),
+        ],
+        scratch_shapes=[pltpu.VMEM((length, 128), F32)],
         compiler_params=params(1, 20),
         name="prepare",
-    )(hidden, hidden, gain[None])
+    )(hidden, hidden, gain[None], w_bc, w_step)
 
 
 def convolve(out, ext, main_ref, before_ref, after_ref, taps_ref):
@@ -156,8 +182,6 @@
     pair = bc_in.shape[2]
     state = pair // 2
     chunks = inner // COLS
-    before_v, before_bc = before[..., :inner], before[..., inner:]
-    after_v, after_bc = after[..., :inner], after[..., inner:]
 
     def at(c):
         return jnp.maximum(c - 1, 0)
@@ -169,9 +193,9 @@
             pl.BlockSpec((1, length, COLS), lambda b, c: (b, 0, at(c))),
             pl.BlockSpec((1, length, pair), lambda b, c: (b, 0, 0)),
             pl.BlockSpec((1, HALO, COLS), lambda b, c: (b, 0, at(c))),
-            pl.BlockSpec((1, HALO, pair), lambda b, c: (b, 0, 0)),
+            pl.BlockSpec((1, HALO, pair), lambda b, c: (b, 0, inner // pair)),
             pl.BlockSpec((1, HALO, COLS), lambda b, c: (b, 0, at(c))),
-            pl.BlockSpec((1, HALO, pair), lambda b, c: (b, 0, 0)),
+            pl.BlockSpec((1, HALO, pair), lambda b, c: (b, 0, inner // pair)),
             pl.BlockSpec((4, COLS), lambda b, c: (0, at(c))),
             pl.BlockSpec((4, pair), lambda b, c: (0, 0)),
             pl.BlockSpec((1, 1) + aux.shape[2:], lambda b, c: (b, at(c), 0, 0)),
@@ -197,7 +221,7 @@
             transcendentals=4 * length * inner,
         ),
         name="mix",
-    )(value_in, bc_in, before_v, before_bc, after_v, after_bc, conv_value, conv_bc, aux, keep)
+    )(value_in, bc_in, before, before, after, after, conv_value, conv_bc, aux, keep)
 
 
 def chain(size, last, local_ref, total_ref, ent_ref, swapped, decay_other, chip, kept,
@@ -577,22 +601,19 @@
     step_bias, decay_rate, skip_gain, out_gain, w_out,
 ):
     keep = (base_ids != 4).astype(F32)[:, None]
-    length, depth = hidden.shape
+    length = hidden.shape[0]
     inner = w_gate.shape[1]
     heads = w_step.shape[1]
     width = inner // heads
     chunks = inner // COLS
     per = COLS // width
-    scaled, squares = prepare(hidden, norm_gain)
-    inv_rms = lax.rsqrt(jnp.sum(squares, axis=-1) / depth + EPSILON)[:, None]
+    scaled, bc_in, step_in, inv_rms = prepare(hidden, norm_gain, w_bc, w_step)
 
     def project(weight):
         return (
             jnp.einsum("btd,dk->btk", scaled, weight, preferred_element_type=F32) * inv_rms
         )
 
-    bc_in = project(w_bc)
-    step_in = project(w_step)
     value_in = project(w_value)
     size = lax.axis_size("ctx")
     up = [(i, i + 1) for i in range(size - 1)]

time: 167 us -> 170 us (1.018)
  Pallas kernels: 102 us -> 109 us
  matrix products: 36.5 us -> 32.7 us
  other arithmetic: 2.45 us -> 4.57 us
    dot_general x4 -> x2, matrix products: 34.5 us -> 28.1 us  [project(): jnp.einsum('btd,dk->btk', scaled, weight, preferred_element_type=F32)]
    pallas_call x1, Pallas kernels: 4.88 us -> 10.1 us  [prepare(): pl.pallas_call(functools.partial(prepare_kernel, depth), grid=(count,), i...]
    slice x4 -> x0, local copies, waits for them, and re-layouts: 3.17 us -> none  [the longest x2 1.6 us: mix(): before_v, before_bc = (before[..., :inner], before[..., inner:])]
    dot_general x1, matrix products: 2.05 us -> 4.62 us  [shards(): cum = jnp.einsum('dts,bsh->bdth', triangles, log_decay, precision=PRECISE)]
    unnamed x49 -> x36, local copies, waits for them, and re-layouts: 11.8 us -> 14.3 us
where the time goes in v5:
time: 170 us; the launch traced here: 169 us
  Pallas kernels  109 us (64%)
  matrix products  32.7 us (19%)
  local copies, waits for them, and re-layouts  18.7 us (11%)
  other arithmetic  4.57 us (3%)
  starting transfers between devices  3.63 us (2%)
    pallas_call x1, Pallas kernels, project_out(): pl.pallas_call(functools.partial(project_out_kernel, count), in_specs=[pl...  37.8 us
    pallas_call x1, Pallas kernels, scan_local(): pl.pallas_call(functools.partial(scan_kernel, size), grid=(2, chunks), in...  34.2 us
    dot_general x2, matrix products, project(): jnp.einsum('btd,dk->btk', scaled, weight, preferred_element_type=F32)  28.1 us
    pallas_call x1, Pallas kernels, mix(): pl.pallas_call(mix_kernel, grid=(2, chunks + 1), in_specs=[pl.BlockSpec((...  19.8 us
    unnamed x36, local copies, waits for them, and re-layouts  14.3 us
    pallas_call x1, Pallas kernels, prepare(): pl.pallas_call(functools.partial(prepare_kernel, depth), grid=(count,), i...  10.1 us
    pallas_call x1, Pallas kernels, finish(): pl.pallas_call(finish_kernel, grid=(2, chunks), in_specs=[pl.BlockSpec((1...  7.33 us
    dot_general x1, matrix products, shards(): cum = jnp.einsum('dts,bsh->bdth', triangles, log_decay, precision=PRECISE)  4.62 us
  transfers between devices with their start and end apart: 2, of which 0 were waited for; matrix products, arithmetic and copies ran while one was open for 17% of the time, Pallas kernels for 0%

profile of v5, /device:TPU:0, one launch (start us, length us, event | category | flops | bytes accessed | tf_op | source)
XLA Modules:
  0.0 169.2 jit_solution(8378696264149718766)
XLA Ops:
  0.0 1.4 copy.32.w_step_ref
  1.4 0.0 copy-start
  1.4 2.2 %copy-done = bf16[512,4096]{1,0:T(8,128)(2,1)S(1)} copy-done((bf16[512,4096]{1,0:T(8,128)(2,1)S(1)}, bf16[512,4096]{1,0:T(8,128)(2,1)}, u32[]{:S(2)}) %copy-start) | copy-done | bytes 4194328
  3.6 1.6 copy-done.4
  5.2 0.7 copy-done.6
  5.9 10.1 %prepare.1 = (bf16[2,512,4096]{2,1,0:T(8,128)(2,1)S(1)}, f32[2,512,256]{2,1,0:T(8,128)S(1)}, f32[2,512,16]{2,1,0:T(8,128)S(1)}, f32[512,1]{1,0:T(8,128)S(1)}) custom-call(bf16[512,4096]{1,0:T(8,128)(2,1)S(1)} %copy-done, bf16[512,4096]{1,0:T(8,128)(2,1)S(1)} %copy-done, f32[1,4096]{1,0:T(1,128)S(1)} %bitcast.48, bf16[4096,256]{1,0:T(8,128)(2,1)S(1)} %copy-done.4, ...), custom_call_target="tpu_custom_call" | custom-call | tf_op jit(solution)/shard_map/prepare/pallas_call | solution.py:99
  16.0 0.0 copy-start.10
  16.0 3.2 %copy-done.10 = bf16[2,512,4096]{2,1,0:T(8,128)(2,1)} copy-done((bf16[2,512,4096]{2,1,0:T(8,128)(2,1)}, bf16[2,512,4096]{2,1,0:T(8,128)(2,1)S(1)}, u32[]{:S(2)}) %copy-start.10) | copy-done | bytes 8388632
  19.3 0.1 reduce
  19.4 0.0 copy-start.14
  19.4 0.0 copy-start.12
  19.4 12.9 %fusion.4.v_ref = f32[2,512,1024]{2,1,0:T(8,128)S(1)} fusion(bf16[2,512,4096]{2,1,0:T(8,128)(2,1)} %copy-done.10, bf16[4096,1024]{1,0:T(8,128)(2,1)} %param.18, f32[512]{0:T(512)S(1)} %reduce), kind=kOutput, calls=%fused_computation.4 | convolution fusion | flops 8590983168 | bytes 20973568 | tf_op jit(solution)/shard_map/btd,dk->btk/dot_general | solution.py:614
  32.4 0.0 copy-start.1
  32.4 2.0 %copy-done.1 = f32[2,512,1024]{2,1,0:T(8,128)} copy-done((f32[2,512,1024]{2,1,0:T(8,128)}, f32[2,512,1024]{2,1,0:T(8,128)S(1)}, u32[]{:S(2)}) %copy-start.1) | copy-done | bytes 4194328
  34.4 0.6 pad_maximum_fusion.1
  35.0 2.3 %collective-permute-start = (f32[2,8,1280]{2,1,0:T(8,128)}, f32[2,8,1280]{2,1,0:T(8,128)S(1)}, u32[]{:S(2)}, u32[]{:S(2)}) collective-permute-start(f32[2,8,1280]{2,1,0:T(8,128)} %pad_maximum_fusion.1), channel_id=1, source_target_pairs={{0,4},{4,8},{8,12},{12,16},{16,20},{20,24},{24,28},{1,5},{5,9},{9,... | collective-permute-start | bytes 245768 | tf_op jit(solution)/shard_map/ppermute | solution.py:623
  37.4 0.6 pad_maximum_fusion.2
  38.0 1.3 collective-permute-start.1
  39.3 1.2 fusion.14
  40.5 0.0 copy-done.14
  40.5 0.0 copy-done.12
  40.5 1.2 fusion.20
  41.7 1.2 copy.40
  42.9 0.2 copy.35
  43.1 4.6 %broadcast_subtract_fusion = (f32[2,2,512,16]{2,3,1,0:T(8,128)S(1)}, f32[2,2,512,16]{2,3,1,0:T(8,128)S(1)}) fusion(f32[2,512,16]{1,2,0:T(8,128)S(1)} %copy.40, f32[1,512,512]{2,1,0:T(8,128)} %get-tuple-element.34, f32[1,512,512]{2,1,0:T(8,128)S(1)} %get-tuple-element.33, f32[2,512,16]{2,1,0:T(8,128)S(1)} %get-tuple-element.26, f32[16]{0:T(128)S(1)} %neg.7), kind=kOutput, calls=%fused_computation.23 | convolution fusion | flops 201900032 | bytes 2490432 | tf_op jit(solution)/shard_map/dts,bsh->bdth/dot_general | solution.py:631
  47.7 0.2 slice_reduce_fusion
  48.0 0.1 broadcast_in_dim.42
  48.0 0.1 broadcast_in_dim_reshape.4.skip_ref
  48.1 0.1 copy.39.keep_ref
  48.3 0.7 reshape.48.row_ref
  49.1 0.1 copy.36
  49.1 0.1 broadcast_in_dim.43
  49.2 0.1 broadcast_in_dim.44
  49.3 15.2 %fusion.7.gate_ref = f32[2,512,1024]{2,1,0:T(8,128)} fusion(bf16[2,512,4096]{2,1,0:T(8,128)(2,1)} %copy-done.10, bf16[4096,1024]{1,0:T(8,128)(2,1)} %param.17, f32[512]{0:T(512)S(1)} %reduce), kind=kOutput, calls=%fused_computation.5 | convolution fusion | flops 8590983168 | bytes 20973568 | tf_op jit(solution)/shard_map/btd,dk->btk/dot_general | solution.py:614
  64.5 0.7 pad_maximum_fusion
  65.2 1.6 copy.38.aux_ref
  66.8 0.0 collective-permute-done.before_v.before_bc
  66.8 0.0 collective-permute-done.1.after_v.after_bc
  66.8 2.2 %copy-done.2 = f32[2,512,1024]{2,1,0:T(8,128)S(1)} copy-done((f32[2,512,1024]{2,1,0:T(8,128)S(1)}, f32[2,512,1024]{2,1,0:T(8,128)}, u32[]{:S(2)}) %copy-start.2) | copy-done | bytes 4194328
  69.0 19.8 %mix.1 = (bf16[2,2,512,1024]{3,2,1,0:T(8,128)(2,1)S(1)}, bf16[2,2,512,256]{3,2,1,0:T(8,128)(2,1)S(1)}, bf16[2,2,128,512]{3,2,1,0:T(8,128)(2,1)S(1)}, f32[2,2,128,1024]{3,2,1,0:T(8,128)S(1)}) custom-call(f32[2,512,1024]{2,1,0:T(8,128)S(1)} %copy-done.2, f32[2,512,256]{2,1,0:T(8,128)S(1)} %get-tuple-element.17.bc_ref, ...), custom_call_target="tpu_custom_call" | custom-call | flops 536870912 | bytes 14680064 | tf_op jit(solution)/shard_map/mix/pallas_call | solution.py:189
  88.8 0.0 copy-start.9
  88.8 0.0 slice-start.1
  88.8 34.2 %scan_local.1 = (f32[2,512,1024]{2,1,0:T(8,128)S(1)}, bf16[2,2,128,1024]{3,2,1,0:T(8,128)(2,1)S(1)}) custom-call(bf16[2,2,512,1024]{3,2,1,0:T(8,128)(2,1)S(1)} %get-tuple-element.19.x_ref, bf16[2,2,512,256]{3,2,1,0:T(8,128)(2,1)S(1)} %get-tuple-element.20.bc_ref, bf16[2,2,128,512]{3,2,1,0:T(8,128)(2,1)S(1)} %get-tuple-element.21.bt_ref, ...), custom_call_target="tpu_custom_call" | custom-call | flops 8589934592 | bytes 10485760 | tf_op jit(solution)/shard_map/scan_local/pallas_call | solution.py:392
  123.1 0.0 copy-done.3
  123.1 0.0 copy-done.9
  123.1 7.3 %finish.1.normed_ref = bf16[2,512,1024]{2,1,0:T(8,128)(2,1)S(1)} custom-call(f32[2,512,1024]{2,1,0:T(8,128)S(1)} %get-tuple-element.23.y_ref, bf16[2,2,512,256]{3,2,1,0:T(8,128)(2,1)S(1)} %get-tuple-element.20.bc_ref, bf16[2,2,128,1024]{3,2,1,0:T(8,128)(2,1)S(1)} %get-tuple-element.24.s_ref, f32[2,4,512,12]{3,2,1,0:T(8,128)S(1)} %copy.38.aux_ref, ...), custom_call_target="tpu_custom_call" | custom-call | tf_op jit(solution)/shard_map/finish/pallas_call | solution.py:468
  130.4 37.8 %project_out.1 = bf16[512,1024]{1,0:T(8,128)(2,1)S(1)} custom-call(bf16[2,512,1024]{2,1,0:T(8,128)(2,1)S(1)} %finish.1.normed_ref, bf16[1024,4096]{1,0:T(8,128)(2,1)S(1)} %bitcast.47), custom_call_target="tpu_custom_call" | custom-call | tf_op jit(solution)/shard_map/project_out/pallas_call | solution.py:580
  168.3 1.0 copy.50
  (27 shorter events, 0.2 us)
Async XLA Ops:
  1.4 2.2 %copy-start = (bf16[512,4096]{1,0:T(8,128)(2,1)S(1)}, bf16[512,4096]{1,0:T(8,128)(2,1)}, u32[]{:S(2)}) copy-start(bf16[512,4096]{1,0:T(8,128)(2,1)} %mirror_ref.1) | copy-start | bytes 12582916
  3.6 1.6 copy-start.4
  5.2 0.7 copy-start.6
  16.0 3.3 %copy-start.10 = (bf16[2,512,4096]{2,1,0:T(8,128)(2,1)}, bf16[2,512,4096]{2,1,0:T(8,128)(2,1)S(1)}, u32[]{:S(2)}) copy-start(bf16[2,512,4096]{2,1,0:T(8,128)(2,1)S(1)} %get-tuple-element.15) | copy-start | bytes 25165828
  19.4 21.1 %copy-start.14 = (f32[16]{0:T(128)S(1)}, f32[16]{0:T(128)}, u32[]{:S(2)}) copy-start(f32[16]{0:T(128)} %param.24) | copy-start | bytes 196
  19.4 21.1 %copy-start.12 = (f32[16]{0:T(128)S(1)}, f32[16]{0:T(128)}, u32[]{:S(2)}) copy-start(f32[16]{0:T(128)} %param.23) | copy-start | bytes 196
  32.4 2.0 %copy-start.1 = (f32[2,512,1024]{2,1,0:T(8,128)}, f32[2,512,1024]{2,1,0:T(8,128)S(1)}, u32[]{:S(2)}) copy-start(f32[2,512,1024]{2,1,0:T(8,128)S(1)} %fusion.4.v_ref) | copy-start | bytes 12582916
  34.4 13.6 %copy-start.11 = (s32[512]{0:T(512)S(1)}, s32[512]{0:T(512)}, u32[]{:S(2)}) copy-start(s32[512]{0:T(512)} %param.15) | copy-start | bytes 6148
  34.4 13.6 %copy-start.13 = (f32[16]{0:T(128)S(1)}, f32[16]{0:T(128)}, u32[]{:S(2)}) copy-start(f32[16]{0:T(128)} %param.25) | copy-start | bytes 196
  35.0 31.7 %collective-permute-start = (f32[2,8,1280]{2,1,0:T(8,128)}, f32[2,8,1280]{2,1,0:T(8,128)S(1)}, u32[]{:S(2)}, u32[]{:S(2)}) collective-permute-start(f32[2,8,1280]{2,1,0:T(8,128)} %pad_maximum_fusion.1), channel_id=1, source_target_pairs={{0,4},{4,8},{8,12},{12,16},{16,20},{20,24},{24,28},{1,5},{5,9},{9,... | collective-permute-start | bytes 245768 | tf_op jit(solution)/shard_map/ppermute | solution.py:623
  38.0 28.8 %collective-permute-start.1 = (f32[2,8,1280]{2,1,0:T(8,128)}, f32[2,8,1280]{2,1,0:T(8,128)}, u32[]{:S(2)}, u32[]{:S(2)}) collective-permute-start(f32[2,8,1280]{2,1,0:T(8,128)} %pad_maximum_fusion.2), channel_id=1, source_target_pairs={{4,0},{8,4},{12,8},{16,12},{20,16},{24,20},{28,24},{5,1},{9,5},{13... | collective-permute-start | bytes 245768 | tf_op jit(solution)/shard_map/ppermute | solution.py:624
  49.3 17.5 %copy-start.7 = (f32[4,1024]{1,0:T(4,128)S(1)}, f32[4,1024]{1,0:T(4,128)}, u32[]{:S(2)}) copy-start(f32[4,1024]{1,0:T(4,128)} %taps_v.1) | copy-start | bytes 49156
  49.3 17.5 %copy-start.8 = (f32[4,256]{1,0:T(4,128)S(1)}, f32[4,256]{1,0:T(4,128)}, u32[]{:S(2)}) copy-start(f32[4,256]{1,0:T(4,128)} %taps_bc.1) | copy-start | bytes 12292
  66.8 2.2 %copy-start.2 = (f32[2,512,1024]{2,1,0:T(8,128)S(1)}, f32[2,512,1024]{2,1,0:T(8,128)}, u32[]{:S(2)}) copy-start(f32[2,512,1024]{2,1,0:T(8,128)} %copy-done.1) | copy-start | bytes 12582916
  69.0 19.8 %copy-start.5 = (f32[2,4,8,512]{3,2,1,0:T(8,128)S(1)}, f32[2,4,8,512]{3,2,1,0:T(8,128)}, u32[]{:S(2)}) copy-start(f32[2,4,8,512]{3,2,1,0:T(8,128)} %reshape.48.row_ref) | copy-start | bytes 393220
  69.0 61.4 %slice-start = ((s8[8388608]{0:T(1024)(128)(4,1)}), s8[4194304]{0:T(1024)(128)(4,1)S(1)}, s32[]{:S(2)}) async-start(s8[8388608]{0:T(1024)(128)(4,1)} %bitcast.46), calls=%async_computation | async-start | bytes 8388608
  88.8 34.3 %copy-start.3 = (f32[2,512,1024]{2,1,0:T(8,128)S(1)}, f32[2,512,1024]{2,1,0:T(8,128)}, u32[]{:S(2)}) copy-start(f32[2,512,1024]{2,1,0:T(8,128)} %fusion.7.gate_ref) | copy-start | bytes 12582916
  88.8 34.3 %copy-start.9 = (f32[1024]{0:T(1024)S(1)}, f32[1024]{0:T(1024)}, u32[]{:S(2)}) copy-start(f32[1024]{0:T(1024)} %param.26) | copy-start | bytes 12292
  88.8 41.6 %slice-start.1 = ((s8[8388608]{0:T(1024)(128)(4,1)}), s8[4194304]{0:T(1024)(128)(4,1)S(1)}, s32[]{:S(2)}) async-start(s8[8388608]{0:T(1024)(128)(4,1)} %bitcast.46), calls=%async_computation.1 | async-start | bytes 8388608
